TPU v7x, 32 devices: a whole 2x2x4 slice. The times are simulated.
32 devices in a mesh: group: 2 (over y), patch: 16 (over z, x, core).
Axes of the slice: x: 2, y: 2, z: 4, core: 2. Of those that a mesh axis runs over, the one named last changes fastest.
Arguments:
- strip_image: bfloat16 [2, 128, 128, 128], P('group', 'patch'), may hold values from -6 to 6
- strip_weight: bfloat16 [2, 128, 128, 128], P('group', 'patch'), may hold values from 0.25 to 4
- strip_patch: int32 [2, 128], P('group', 'patch'), may hold values from 0 to 15, as said below
- strip_slot: int32 [2, 128], P('group', 'patch'), may hold values from 0 to 7, as said below
- kernel_coef: float32 [2, 16, 2, 3, 31], P('group', 'patch'), may hold values from -5 to 5
Outputs:
- coadd: float32 [16, 128, 512], P('patch', 'group')
Inputs may be any that keep to these rules, and one draw needn't show every extreme that they name: `strip_patch`: within a group, each device sends at most 1 of its strips to any one patch and sends exactly 1 to some patch; every patch receives exactly 8 strips of each group. `strip_slot`: within a group, the 8 strips on one patch carry each slot number once.
All inputs are finite; a program needn't handle non-finite values.
Results may differ from a plain program's by a relative error of at most 0.0051.
Values may be sent and summed in bfloat16 or wider, within the bound.
A program may use at most 128 MiB of HBM per device.

v0:
```python
import jax
import jax.numpy as jnp
from jax import lax
from jax.sharding import PartitionSpec as P

TAPS = 23


SPREADS = (0.7, 1.5, 3.0)
DEGREES = (4, 3, 2)


def profile_table(tap_count):
    half_width = (tap_count - 1) // 2
    offsets = jnp.arange(-half_width, half_width + 1).astype(jnp.float32)
    profiles = []
    for spread, degree in zip(SPREADS, DEGREES):
        for exponent in range(degree + 1):
            profile = (
                jnp.exp(-offsets * offsets / (2.0 * spread * spread))
                * (offsets / spread) ** exponent
            )
            profiles.append(profile / jnp.sqrt(jnp.sum(profile * profile)))
    return jnp.stack(profiles)


def basis_pairs():
    vertical_list = []
    horizontal_list = []
    start_index = 0
    for degree in DEGREES:
        for vertical in range(degree + 1):
            for horizontal in range(degree + 1 - vertical):
                vertical_list.append(start_index + vertical)
                horizontal_list.append(start_index + horizontal)
        start_index += degree + 1
    return (vertical_list, horizontal_list)


def band_between(profile, inputs, outputs):
    half_width = (profile.shape[0] - 1) // 2
    differ = outputs[None, :] - inputs[:, None]
    inside = jnp.abs(differ) <= half_width
    picked = jnp.take(profile, jnp.clip(differ + half_width, 0, 2 * half_width), axis=0)
    return jnp.where(inside, picked, jnp.zeros_like(picked))


def per_device(strip_image, strip_weight, strip_patch, strip_slot, kernel_coef):
    patch_count = lax.axis_size("patch")
    group_count = lax.axis_size("group")
    strip_count = strip_image.shape[1]
    row_count = strip_image.shape[2]
    strip_width = strip_image.shape[3]
    visits = kernel_coef.shape[2]
    blocks = strip_count // visits
    capacity = max(1, 2 * strip_count // patch_count)
    slot_count = patch_count * capacity
    profiles = profile_table(TAPS).astype(jnp.bfloat16)
    profile_count = profiles.shape[0]
    half_width = (TAPS - 1) // 2
    row_axis = jnp.arange(row_count, dtype=jnp.int32)
    row_stack = jnp.stack(
        [
            band_between(profiles[profile_index], row_axis, row_axis).T
            for profile_index in range(profile_count)
        ]
    )
    images = strip_image[0]
    weights = strip_weight[0]
    targets = strip_patch[0]
    labels = strip_slot[0]
    counter = jnp.arange(strip_count, dtype=jnp.int32)
    same_target = targets[:, None] == targets[None, :]
    earlier = counter[None, :] < counter[:, None]
    ranking = jnp.sum((same_target & earlier).astype(jnp.int32), axis=1)
    placing = targets * capacity + ranking
    matched = placing[None, :] == jnp.arange(slot_count, dtype=jnp.int32)[:, None]
    source = jnp.sum(jnp.where(matched, counter[None, :], 0), axis=1)
    filled = jnp.any(matched, axis=1)
    send_image = jnp.where(
        filled[:, None, None], jnp.take(images, source, axis=0), jnp.zeros((), jnp.bfloat16)
    )
    send_weight = jnp.where(
        filled[:, None, None], jnp.take(weights, source, axis=0), jnp.zeros((), jnp.bfloat16)
    )
    send_label = jnp.where(filled, jnp.take(labels, source) + 1, 0).astype(jnp.bfloat16)
    wanted = jnp.arange(strip_count, dtype=jnp.int32) + 1
    got_image, got_weight, got_label = (
        lax.all_to_all(send_image, "patch", split_axis=0, concat_axis=0, tiled=True),
        lax.all_to_all(send_weight, "patch", split_axis=0, concat_axis=0, tiled=True),
        lax.all_to_all(send_label, "patch", split_axis=0, concat_axis=0, tiled=True),
    )
    located = got_label.astype(jnp.int32)[None, :] == wanted[:, None]
    position = jnp.sum(
        jnp.where(located, jnp.arange(slot_count, dtype=jnp.int32)[None, :], 0), axis=1
    )
    patch_image = jnp.take(got_image, position, axis=0).reshape(
        visits, blocks, row_count, strip_width
    )
    patch_weight = jnp.take(got_weight, position, axis=0).reshape(
        visits, blocks, row_count, strip_width
    )
    vertical_list, horizontal_list = basis_pairs()
    col_axis = jnp.arange(strip_width, dtype=jnp.int32)
    tail_axis = jnp.arange(half_width, dtype=jnp.int32) - half_width
    head_axis = jnp.arange(half_width, dtype=jnp.int32) + strip_width
    member_lists = []
    middle_bands = []
    lower_bands = []
    upper_bands = []
    for profile_index in range(profile_count):
        members = [
            basis for basis in range(len(vertical_list)) if vertical_list[basis] == profile_index
        ]
        member_lists.append(jnp.asarray(members, dtype=jnp.int32))
        middle_bands.append(
            jnp.concatenate(
                [
                    band_between(profiles[horizontal_list[basis]], col_axis, col_axis)
                    for basis in members
                ],
                axis=1,
            )
        )
        lower_bands.append(
            jnp.concatenate(
                [
                    band_between(profiles[horizontal_list[basis]], tail_axis, col_axis)
                    for basis in members
                ],
                axis=1,
            )
        )
        upper_bands.append(
            jnp.concatenate(
                [
                    band_between(profiles[horizontal_list[basis]], head_axis, col_axis)
                    for basis in members
                ],
                axis=1,
            )
        )
    patch_cols = blocks * strip_width
    across = (2.0 * jnp.arange(patch_cols).astype(jnp.float32) - (patch_cols - 1)) / (
        patch_cols - 1
    )
    across = across.reshape(blocks, strip_width)
    downward = (2.0 * jnp.arange(row_count).astype(jnp.float32) - (row_count - 1)) / (row_count - 1)
    edge_zero = jnp.zeros((1, row_count, half_width), jnp.bfloat16)

    def visit_step(running, visit_item):
        block_source, block_weight, visit_coef = visit_item
        row_pass = jnp.einsum(
            "qzy,kys->qkzs", row_stack, block_source, preferred_element_type=jnp.float32
        ).astype(jnp.bfloat16)
        picture = jnp.zeros((blocks, row_count, strip_width), jnp.float32)
        for profile_index in range(profile_count):
            members = member_lists[profile_index]
            current = row_pass[profile_index]
            tail_cols = jnp.concatenate(
                [edge_zero, current[:-1, :, strip_width - half_width :]], axis=0
            )
            head_cols = jnp.concatenate([current[1:, :, :half_width], edge_zero], axis=0)
            result = jnp.einsum(
                "kys,st->kyt",
                current,
                middle_bands[profile_index],
                preferred_element_type=jnp.float32,
            )
            result = result + jnp.einsum(
                "kyh,ht->kyt",
                tail_cols,
                lower_bands[profile_index],
                preferred_element_type=jnp.float32,
            )
            result = result + jnp.einsum(
                "kyh,ht->kyt",
                head_cols,
                upper_bands[profile_index],
                preferred_element_type=jnp.float32,
            )
            result = result.reshape(blocks, row_count, members.shape[0], strip_width)
            chosen = visit_coef[:, members]
            spatial = (
                chosen[0][None, None, :, None]
                + chosen[1][None, None, :, None] * across[:, None, None, :]
                + chosen[2][None, None, :, None] * downward[None, :, None, None]
            )
            picture = picture + jnp.sum(result * spatial, axis=2)
        inverse_var = block_weight.astype(jnp.float32)
        return ((running[0] + inverse_var * picture, running[1] + inverse_var), None)

    zeros_field = jnp.zeros((blocks, row_count, strip_width), jnp.float32)
    (numerator, denominator), _ = lax.scan(
        visit_step, (zeros_field, zeros_field), (patch_image, patch_weight, kernel_coef[0, 0])
    )
    slab_rows = row_count // group_count
    moved_numer, moved_denom = (
        lax.all_to_all(numerator, "group", split_axis=1, concat_axis=0, tiled=True),
        lax.all_to_all(denominator, "group", split_axis=1, concat_axis=0, tiled=True),
    )
    numer_share = jnp.sum(moved_numer.reshape(group_count, blocks, slab_rows, strip_width), axis=0)
    denom_share = jnp.sum(moved_denom.reshape(group_count, blocks, slab_rows, strip_width), axis=0)
    coadded = numer_share / denom_share
    return jnp.transpose(coadded, (1, 0, 2)).reshape(1, slab_rows, patch_cols)


def solution(mesh):
    return jax.shard_map(
        per_device,
        mesh=mesh,
        in_specs=(
            P("group", "patch", None, None),
            P("group", "patch", None, None),
            P("group", "patch"),
            P("group", "patch"),
            P("group", "patch", None, None, None),
        ),
        out_specs=P("patch", "group", None),
        check_vma=False,
    )
```

profile of v0, /device:TPU:0, one launch (start us, length us, event | category | flops | bytes accessed | tf_op | source)
XLA Modules:
  0.0 924.3 jit_solution(7800853028019453611)
XLA Ops:
  44.2 14.3 %constant_dynamic-update-slice_fusion.11 = bf16[12,128,128]{1,2,0:T(8,128)(2,1)S(1)} fusion(bf16[]{:T(256)} %bitcast.36, bf16[]{:T(256)} %bitcast.35, bf16[]{:T(256)} %bitcast.34, bf16[]{:T(256)} %bitcast.33, bf16[]{:T(256)} %bitcast.32, bf16[]{:T(256)} %bitcast.31, bf16[]{:T(256)} %bitcast.30, bf16[]{:T(256)} %bitcast.29, bf16[]{:T(256)} %bitcast.28, ...), kind=kLoop, calls=%fused_computation.305 | loop fusion | flops 933887 | bytes 32814
  58.5 14.9 %select_select_fusion.13 = bf16[128,128]{1,0:T(8,128)(2,1)} fusion(bf16[]{:T(256)} %bitcast.36, bf16[]{:T(256)} %bitcast.35, bf16[]{:T(256)} %bitcast.34, bf16[]{:T(256)} %bitcast.33, bf16[]{:T(256)} %bitcast.32, bf16[]{:T(256)} %bitcast.31, bf16[]{:T(256)} %bitcast.30, bf16[]{:T(256)} %bitcast.29, bf16[]{:T(256)} %bitcast.28, bf16[]{:T(256)} %bitcast.27, ...), kind=kLoop, calls=%fused_computation.332 | loop fusion | flops 933888 | bytes 32814 | tf_op jit(solution)/shard_map/jit(_where)/select_n | solution.py:45
  73.6 8.3 gather_fusion.14
  81.9 8.3 gather_fusion.15
  90.3 8.3 gather_fusion.16
  98.6 8.3 gather_fusion.24
  107.0 8.3 gather_fusion.25
  115.3 8.3 gather_fusion.26
  123.7 8.3 gather_fusion.27
  132.0 8.3 gather_fusion.32
  140.4 8.3 gather_fusion.33
  148.7 8.3 gather_fusion.34
  157.1 8.3 gather_fusion.19
  165.4 8.3 gather_fusion.20
  173.7 8.3 gather_fusion.21
  223.8 8.3 gather_fusion.36
  232.2 8.3 gather_fusion.37
  240.5 14.9 %constant_dynamic-update-slice_fusion.16 = bf16[128,640]{1,0:T(8,128)(2,1)} fusion(bf16[]{:T(256)} %bitcast.36, bf16[]{:T(256)} %bitcast.35, bf16[]{:T(256)} %bitcast.34, bf16[]{:T(256)} %bitcast.33, bf16[]{:T(256)} %bitcast.32, bf16[]{:T(256)} %bitcast.31, bf16[]{:T(256)} %bitcast.30, bf16[]{:T(256)} %bitcast.29, bf16[]{:T(256)} %bitcast.28, bf16[]{:T(256)} %bitcast.27, ...), kind=kLoop, calls=%fused_computation.310 | loop fusion | flops 933887 | bytes 32814
  263.8 8.3 gather_fusion.22
  272.1 8.3 gather_fusion.18
  280.5 8.6 gather_fusion.23
  289.1 14.3 %select_select_fusion.12 = bf16[128,128]{1,0:T(8,128)(2,1)S(1)} fusion(bf16[]{:T(256)} %bitcast.62, bf16[]{:T(256)} %bitcast.61, bf16[]{:T(256)} %bitcast.60, bf16[]{:T(256)} %bitcast.59, bf16[]{:T(256)} %bitcast.58, bf16[]{:T(256)} %bitcast.57, bf16[]{:T(256)} %bitcast.56, bf16[]{:T(256)} %bitcast.55, bf16[]{:T(256)} %bitcast.54, bf16[]{:T(256)} %bitcast.53, ...), kind=kLoop, calls=%fused_computation.331 | loop fusion | flops 933888 | bytes 32814 | tf_op jit(solution)/shard_map/jit(_where)/select_n | solution.py:45
  303.4 14.3 %constant_dynamic-update-slice_fusion.10 = bf16[12,128,128]{1,2,0:T(8,128)(2,1)S(1)} fusion(bf16[12,128,128]{1,2,0:T(8,128)(2,1)S(1)} %constant_dynamic-update-slice_fusion.11, bf16[]{:T(256)} %bitcast.62, bf16[]{:T(256)} %bitcast.61, bf16[]{:T(256)} %bitcast.60, bf16[]{:T(256)} %bitcast.59, bf16[]{:T(256)} %bitcast.58, bf16[]{:T(256)} %bitcast.57, ...), kind=kLoop, calls=%fused_computation.304 | loop fusion | flops 933888 | bytes 32814
  317.7 14.6 %select_select_fusion.11 = bf16[128,128]{1,0:T(8,128)(2,1)S(1)} fusion(bf16[]{:T(256)} %bitcast.88, bf16[]{:T(256)} %bitcast.87, bf16[]{:T(256)} %bitcast.86, bf16[]{:T(256)} %bitcast.85, bf16[]{:T(256)} %bitcast.84, bf16[]{:T(256)} %bitcast.83, bf16[]{:T(256)} %bitcast.82, bf16[]{:T(256)} %bitcast.81, bf16[]{:T(256)} %bitcast.80, bf16[]{:T(256)} %bitcast.79, ...), kind=kLoop, calls=%fused_computation.330 | loop fusion | flops 933888 | bytes 32814 | tf_op jit(solution)/shard_map/jit(_where)/select_n | solution.py:45
  332.3 14.6 %constant_dynamic-update-slice_fusion.9 = bf16[12,128,128]{1,2,0:T(8,128)(2,1)S(1)} fusion(bf16[12,128,128]{1,2,0:T(8,128)(2,1)S(1)} %constant_dynamic-update-slice_fusion.10, bf16[]{:T(256)} %bitcast.88, bf16[]{:T(256)} %bitcast.87, bf16[]{:T(256)} %bitcast.86, bf16[]{:T(256)} %bitcast.85, bf16[]{:T(256)} %bitcast.84, bf16[]{:T(256)} %bitcast.83, ...), kind=kLoop, calls=%fused_computation.303 | loop fusion | flops 933888 | bytes 32814
  346.9 14.5 %select_select_fusion.10 = bf16[128,128]{1,0:T(8,128)(2,1)S(1)} fusion(bf16[]{:T(256)} %bitcast.114, bf16[]{:T(256)} %bitcast.113, bf16[]{:T(256)} %bitcast.112, bf16[]{:T(256)} %bitcast.111, bf16[]{:T(256)} %bitcast.110, bf16[]{:T(256)} %bitcast.109, bf16[]{:T(256)} %bitcast.108, bf16[]{:T(256)} %bitcast.107, bf16[]{:T(256)} %bitcast.106, bf16[]{:T(256)} %bitcast.105, ...), kind=kLoop, calls=%fused_computation.329 | loop fusion | flops 933888 | bytes 32814 | tf_op jit(solution)/shard_map/jit(_where)/select_n | solution.py:45
  361.4 14.5 %constant_dynamic-update-slice_fusion.8 = bf16[12,128,128]{1,2,0:T(8,128)(2,1)S(1)} fusion(bf16[12,128,128]{1,2,0:T(8,128)(2,1)S(1)} %constant_dynamic-update-slice_fusion.9, bf16[]{:T(256)} %bitcast.114, bf16[]{:T(256)} %bitcast.113, bf16[]{:T(256)} %bitcast.112, bf16[]{:T(256)} %bitcast.111, bf16[]{:T(256)} %bitcast.110, bf16[]{:T(256)} %bitcast.109, ...), kind=kLoop, calls=%fused_computation.302 | loop fusion | flops 933888 | bytes 32814
  375.8 14.9 %select_select_fusion.8 = bf16[128,128]{1,0:T(8,128)(2,1)} fusion(bf16[]{:T(256)} %bitcast.166, bf16[]{:T(256)} %bitcast.165, bf16[]{:T(256)} %bitcast.164, bf16[]{:T(256)} %bitcast.163, bf16[]{:T(256)} %bitcast.162, bf16[]{:T(256)} %bitcast.161, bf16[]{:T(256)} %bitcast.160, bf16[]{:T(256)} %bitcast.159, bf16[]{:T(256)} %bitcast.158, bf16[]{:T(256)} %bitcast.157, ...), kind=kLoop, calls=%fused_computation.327 | loop fusion | flops 933888 | bytes 32814 | tf_op jit(solution)/shard_map/jit(_where)/select_n | solution.py:45
  390.8 14.6 %constant_dynamic-update-slice_fusion.7 = bf16[12,128,128]{1,2,0:T(8,128)(2,1)S(1)} fusion(bf16[12,128,128]{1,2,0:T(8,128)(2,1)S(1)} %constant_dynamic-update-slice_fusion.8, bf16[]{:T(256)} %bitcast.140, bf16[]{:T(256)} %bitcast.139, bf16[]{:T(256)} %bitcast.138, bf16[]{:T(256)} %bitcast.137, bf16[]{:T(256)} %bitcast.136, bf16[]{:T(256)} %bitcast.135, ...), kind=kLoop, calls=%fused_computation.301 | loop fusion | flops 933888 | bytes 32814
  405.4 14.4 %constant_dynamic-update-slice_fusion.6 = bf16[12,128,128]{1,2,0:T(8,128)(2,1)S(1)} fusion(bf16[12,128,128]{1,2,0:T(8,128)(2,1)S(1)} %constant_dynamic-update-slice_fusion.7, bf16[]{:T(256)} %bitcast.166, bf16[]{:T(256)} %bitcast.165, bf16[]{:T(256)} %bitcast.164, bf16[]{:T(256)} %bitcast.163, bf16[]{:T(256)} %bitcast.162, bf16[]{:T(256)} %bitcast.161, ...), kind=kLoop, calls=%fused_computation.300 | loop fusion | flops 933888 | bytes 32814
  419.7 14.6 %select_select_fusion.7 = bf16[128,128]{1,0:T(8,128)(2,1)S(1)} fusion(bf16[]{:T(256)} %bitcast.192, bf16[]{:T(256)} %bitcast.191, bf16[]{:T(256)} %bitcast.190, bf16[]{:T(256)} %bitcast.189, bf16[]{:T(256)} %bitcast.188, bf16[]{:T(256)} %bitcast.187, bf16[]{:T(256)} %bitcast.186, bf16[]{:T(256)} %bitcast.185, bf16[]{:T(256)} %bitcast.184, bf16[]{:T(256)} %bitcast.183, ...), kind=kLoop, calls=%fused_computation.326 | loop fusion | flops 933888 | bytes 32814 | tf_op jit(solution)/shard_map/jit(_where)/select_n | solution.py:45
  434.3 14.6 %constant_dynamic-update-slice_fusion.5 = bf16[12,128,128]{1,2,0:T(8,128)(2,1)S(1)} fusion(bf16[12,128,128]{1,2,0:T(8,128)(2,1)S(1)} %constant_dynamic-update-slice_fusion.6, bf16[]{:T(256)} %bitcast.192, bf16[]{:T(256)} %bitcast.191, bf16[]{:T(256)} %bitcast.190, bf16[]{:T(256)} %bitcast.189, bf16[]{:T(256)} %bitcast.188, bf16[]{:T(256)} %bitcast.187, ...), kind=kLoop, calls=%fused_computation.299 | loop fusion | flops 933888 | bytes 32814
  448.9 14.2 %select_select_fusion.6 = bf16[128,128]{1,0:T(8,128)(2,1)S(1)} fusion(bf16[]{:T(256)} %bitcast.218, bf16[]{:T(256)} %bitcast.217, bf16[]{:T(256)} %bitcast.216, bf16[]{:T(256)} %bitcast.215, bf16[]{:T(256)} %bitcast.214, bf16[]{:T(256)} %bitcast.213, bf16[]{:T(256)} %bitcast.212, bf16[]{:T(256)} %bitcast.211, bf16[]{:T(256)} %bitcast.210, bf16[]{:T(256)} %bitcast.209, ...), kind=kLoop, calls=%fused_computation.325 | loop fusion | flops 933888 | bytes 32814 | tf_op jit(solution)/shard_map/jit(_where)/select_n | solution.py:45
  463.1 14.2 %constant_dynamic-update-slice_fusion.4 = bf16[12,128,128]{1,2,0:T(8,128)(2,1)S(1)} fusion(bf16[12,128,128]{1,2,0:T(8,128)(2,1)S(1)} %constant_dynamic-update-slice_fusion.5, bf16[]{:T(256)} %bitcast.218, bf16[]{:T(256)} %bitcast.217, bf16[]{:T(256)} %bitcast.216, bf16[]{:T(256)} %bitcast.215, bf16[]{:T(256)} %bitcast.214, bf16[]{:T(256)} %bitcast.213, ...), kind=kLoop, calls=%fused_computation.298 | loop fusion | flops 933888 | bytes 32814
  477.4 14.6 %select_select_fusion.5 = bf16[128,128]{1,0:T(8,128)(2,1)S(1)} fusion(bf16[]{:T(256)} %bitcast.244, bf16[]{:T(256)} %bitcast.243, bf16[]{:T(256)} %bitcast.242, bf16[]{:T(256)} %bitcast.241, bf16[]{:T(256)} %bitcast.240, bf16[]{:T(256)} %bitcast.239, bf16[]{:T(256)} %bitcast.238, bf16[]{:T(256)} %bitcast.237, bf16[]{:T(256)} %bitcast.236, bf16[]{:T(256)} %bitcast.235, ...), kind=kLoop, calls=%fused_computation.324 | loop fusion | flops 933888 | bytes 32814 | tf_op jit(solution)/shard_map/jit(_where)/select_n | solution.py:45
  492.0 14.6 %constant_dynamic-update-slice_fusion.3 = bf16[12,128,128]{1,2,0:T(8,128)(2,1)S(1)} fusion(bf16[12,128,128]{1,2,0:T(8,128)(2,1)S(1)} %constant_dynamic-update-slice_fusion.4, bf16[]{:T(256)} %bitcast.244, bf16[]{:T(256)} %bitcast.243, bf16[]{:T(256)} %bitcast.242, bf16[]{:T(256)} %bitcast.241, bf16[]{:T(256)} %bitcast.240, bf16[]{:T(256)} %bitcast.239, ...), kind=kLoop, calls=%fused_computation.297 | loop fusion | flops 933888 | bytes 32814
  506.6 15.1 %select_select_fusion.4 = bf16[128,128]{1,0:T(8,128)(2,1)} fusion(bf16[]{:T(256)} %bitcast.270, bf16[]{:T(256)} %bitcast.269, bf16[]{:T(256)} %bitcast.268, bf16[]{:T(256)} %bitcast.267, bf16[]{:T(256)} %bitcast.266, bf16[]{:T(256)} %bitcast.265, bf16[]{:T(256)} %bitcast.264, bf16[]{:T(256)} %bitcast.263, bf16[]{:T(256)} %bitcast.262, bf16[]{:T(256)} %bitcast.261, ...), kind=kLoop, calls=%fused_computation.323 | loop fusion | flops 933888 | bytes 32814 | tf_op jit(solution)/shard_map/jit(_where)/select_n | solution.py:45
  521.7 14.5 %constant_dynamic-update-slice_fusion.2 = bf16[12,128,128]{1,2,0:T(8,128)(2,1)S(1)} fusion(bf16[12,128,128]{1,2,0:T(8,128)(2,1)S(1)} %constant_dynamic-update-slice_fusion.3, bf16[]{:T(256)} %bitcast.270, bf16[]{:T(256)} %bitcast.269, bf16[]{:T(256)} %bitcast.268, bf16[]{:T(256)} %bitcast.267, bf16[]{:T(256)} %bitcast.266, bf16[]{:T(256)} %bitcast.265, ...), kind=kLoop, calls=%fused_computation.296 | loop fusion | flops 933888 | bytes 32814
  536.2 14.4 %select_select_fusion.3 = bf16[128,128]{1,0:T(8,128)(2,1)S(1)} fusion(bf16[]{:T(256)} %bitcast.296, bf16[]{:T(256)} %bitcast.295, bf16[]{:T(256)} %bitcast.294, bf16[]{:T(256)} %bitcast.293, bf16[]{:T(256)} %bitcast.292, bf16[]{:T(256)} %bitcast.291, bf16[]{:T(256)} %bitcast.290, bf16[]{:T(256)} %bitcast.289, bf16[]{:T(256)} %bitcast.288, bf16[]{:T(256)} %bitcast.287, ...), kind=kLoop, calls=%fused_computation.322 | loop fusion | flops 933888 | bytes 32814 | tf_op jit(solution)/shard_map/jit(_where)/select_n | solution.py:45
  550.6 14.4 %constant_dynamic-update-slice_fusion.1 = bf16[12,128,128]{1,2,0:T(8,128)(2,1)S(1)} fusion(bf16[12,128,128]{1,2,0:T(8,128)(2,1)S(1)} %constant_dynamic-update-slice_fusion.2, bf16[]{:T(256)} %bitcast.296, bf16[]{:T(256)} %bitcast.295, bf16[]{:T(256)} %bitcast.294, bf16[]{:T(256)} %bitcast.293, bf16[]{:T(256)} %bitcast.292, bf16[]{:T(256)} %bitcast.291, ...), kind=kLoop, calls=%fused_computation.295 | loop fusion | flops 933888 | bytes 32814
  565.0 14.5 %select_select_fusion.2 = bf16[128,128]{1,0:T(8,128)(2,1)S(1)} fusion(bf16[]{:T(256)} %bitcast.322, bf16[]{:T(256)} %bitcast.321, bf16[]{:T(256)} %bitcast.320, bf16[]{:T(256)} %bitcast.319, bf16[]{:T(256)} %bitcast.318, bf16[]{:T(256)} %bitcast.317, bf16[]{:T(256)} %bitcast.316, bf16[]{:T(256)} %bitcast.315, bf16[]{:T(256)} %bitcast.314, bf16[]{:T(256)} %bitcast.313, ...), kind=kLoop, calls=%fused_computation.321 | loop fusion | flops 933888 | bytes 32814 | tf_op jit(solution)/shard_map/jit(_where)/select_n | solution.py:45
  579.5 14.5 %constant_dynamic-update-slice_fusion = bf16[12,128,128]{1,2,0:T(8,128)(2,1)S(1)} fusion(bf16[12,128,128]{1,2,0:T(8,128)(2,1)S(1)} %constant_dynamic-update-slice_fusion.1, bf16[]{:T(256)} %bitcast.322, bf16[]{:T(256)} %bitcast.321, bf16[]{:T(256)} %bitcast.320, bf16[]{:T(256)} %bitcast.319, bf16[]{:T(256)} %bitcast.318, bf16[]{:T(256)} %bitcast.317, ...), kind=kLoop, calls=%fused_computation.294 | loop fusion | flops 933888 | bytes 32814 | tf_op jit(solution)/shard_map/stack | solution.py:62
  605.5 14.9 %constant_dynamic-update-slice_fusion.15 = bf16[128,640]{1,0:T(8,128)(2,1)} fusion(bf16[128,640]{1,0:T(8,128)(2,1)} %constant_dynamic-update-slice_fusion.16, bf16[]{:T(256)} %bitcast.62, bf16[]{:T(256)} %bitcast.61, bf16[]{:T(256)} %bitcast.60, bf16[]{:T(256)} %bitcast.59, bf16[]{:T(256)} %bitcast.58, bf16[]{:T(256)} %bitcast.57, bf16[]{:T(256)} %bitcast.56, ...), kind=kLoop, calls=%fused_computation.309 | loop fusion | flops 933888 | bytes 44544
  620.4 15.2 %constant_dynamic-update-slice_fusion.14 = bf16[128,640]{1,0:T(8,128)(2,1)} fusion(bf16[128,640]{1,0:T(8,128)(2,1)} %constant_dynamic-update-slice_fusion.15, bf16[]{:T(256)} %bitcast.88, bf16[]{:T(256)} %bitcast.87, bf16[]{:T(256)} %bitcast.86, bf16[]{:T(256)} %bitcast.85, bf16[]{:T(256)} %bitcast.84, bf16[]{:T(256)} %bitcast.83, bf16[]{:T(256)} %bitcast.82, ...), kind=kLoop, calls=%fused_computation.308 | loop fusion | flops 933888 | bytes 44544
  635.6 15.1 %constant_dynamic-update-slice_fusion.13 = bf16[128,640]{1,0:T(8,128)(2,1)} fusion(bf16[128,640]{1,0:T(8,128)(2,1)} %constant_dynamic-update-slice_fusion.14, bf16[]{:T(256)} %bitcast.114, bf16[]{:T(256)} %bitcast.113, bf16[]{:T(256)} %bitcast.112, bf16[]{:T(256)} %bitcast.111, bf16[]{:T(256)} %bitcast.110, bf16[]{:T(256)} %bitcast.109, bf16[]{:T(256)} %bitcast.108, ...), kind=kLoop, calls=%fused_computation.307 | loop fusion | flops 933888 | bytes 44544
  673.5 15.2 %constant_dynamic-update-slice_fusion.12 = bf16[128,640]{1,0:T(8,128)(2,1)} fusion(bf16[128,640]{1,0:T(8,128)(2,1)} %constant_dynamic-update-slice_fusion.13, bf16[]{:T(256)} %bitcast.140, bf16[]{:T(256)} %bitcast.139, bf16[]{:T(256)} %bitcast.138, bf16[]{:T(256)} %bitcast.137, bf16[]{:T(256)} %bitcast.136, bf16[]{:T(256)} %bitcast.135, bf16[]{:T(256)} %bitcast.134, ...), kind=kLoop, calls=%fused_computation.306 | loop fusion | flops 933888 | bytes 44544 | tf_op jit(solution)/shard_map/concatenate | solution.py:117
  703.8 12.6 %all-to-all-done.2 = bf16[16,128,128]{2,1,0:T(8,128)(2,1)S(1)} async-done(((bf16[16,128,128]{2,1,0:T(8,128)(2,1)}), bf16[16,128,128]{2,1,0:T(8,128)(2,1)S(1)}, u32[]{:S(2)}, u32[]{:S(2)}) %all-to-all-start.2) | async-done | bytes 524320 | tf_op jit(solution)/shard_map/all_to_all | solution.py:89
  718.7 185.1 %while.29 = (s32[]{:T(128)}, f32[4,128,128]{2,1,0:T(8,128)}, f32[4,128,128]{2,1,0:T(8,128)}, bf16[2,4,128,128]{3,2,1,0:T(8,128)(2,1)}, bf16[2,4,128,128]{2,3,1,0...) while((s32[]{:T(128)}, f32[4,128,128]{2,1,0:T(8,128)}, ...), condition=%wide.region_26.31_spmd.clone.clone.clone, body=%wide.region_16.30_spmd.sunk.clone.clone.clone.sunk | while | flops 799856128 | bytes 87721488 | solution.py:194
  (513 shorter events, 326.1 us)
Async XLA Ops:
  0.0 664.2 %copy-start = (bf16[1,8,128,128]{3,2,1,0:T(8,128)(2,1)S(1)}, bf16[1,8,128,128]{3,2,1,0:T(8,128)(2,1)}, u32[]{:S(2)}) copy-start(bf16[1,8,128,128]{3,2,1,0:T(8,128)(2,1)} %param.28) | copy-start | bytes 786436
  3.8 663.7 %all-to-all-start.1 = ((bf16[16,1,1]{2,1,0:T(2,128)(2,1)}), bf16[16,1,1]{2,1,0:T(2,128)(2,1)S(1)}, u32[]{:S(2)}, u32[]{:S(2)}) async-start(bf16[16,1,1]{2,1,0:T(2,128)(2,1)} %copy.179), calls=%async_computation.1 | async-start | bytes 16384 | tf_op jit(solution)/shard_map/all_to_all | solution.py:91
  506.6 158.3 %copy-start.14 = (bf16[1,8,128,128]{3,2,1,0:T(8,128)(2,1)S(1)}, bf16[1,8,128,128]{3,2,1,0:T(8,128)(2,1)}, u32[]{:S(2)}) copy-start(bf16[1,8,128,128]{3,2,1,0:T(8,128)(2,1)} %param.27) | copy-start | bytes 786436
  595.0 70.5 %copy-start.41 = (f32[1,1,2,3,31]{4,2,3,1,0:T(2,128)S(1)}, f32[1,1,2,3,31]{4,2,3,1,0:T(2,128)}, u32[]{:S(2)}) copy-start(f32[1,1,2,3,31]{4,2,3,1,0:T(2,128)} %param.31) | copy-start | bytes 2236
  667.5 28.5 %all-to-all-start = ((bf16[16,128,128]{2,1,0:T(8,128)(2,1)}), bf16[16,128,128]{2,1,0:T(8,128)(2,1)S(1)}, u32[]{:S(2)}, u32[]{:S(2)}) async-start(bf16[16,128,128]{2,1,0:T(8,128)(2,1)} %get-tuple-element.1631), calls=%async_computation | async-start | bytes 1048576 | tf_op jit(solution)/shard_map/all_to_all | solution.py:90
  695.9 20.5 %all-to-all-start.2 = ((bf16[16,128,128]{2,1,0:T(8,128)(2,1)}), bf16[16,128,128]{2,1,0:T(8,128)(2,1)S(1)}, u32[]{:S(2)}, u32[]{:S(2)}) async-start(bf16[16,128,128]{2,1,0:T(8,128)(2,1)} %get-tuple-element.1630), calls=%async_computation.2 | async-start | bytes 1048576 | tf_op jit(solution)/shard_map/all_to_all | solution.py:89
  730.0 4.3 copy-start.17
  730.0 8.4 copy-start.19
  730.0 23.3 %copy-start.7 = (bf16[128,384]{1,0:T(8,128)(2,1)}, bf16[128,384]{1,0:T(8,128)(2,1)S(1)}, u32[]{:S(2)}) copy-start(bf16[128,384]{1,0:T(8,128)(2,1)S(1)} %get-tuple-element.2479) | copy-start | bytes 294916 | tf_op jit(solution)/shard_map/while
  732.7 20.9 %copy-start.6 = (bf16[4,128,128]{1,2,0:T(8,128)(2,1)}, bf16[4,128,128]{1,2,0:T(8,128)(2,1)S(1)}, u32[]{:S(2)}) copy-start(bf16[4,128,128]{1,2,0:T(8,128)(2,1)S(1)} %get-tuple-element.2280) | copy-start | bytes 393220 | tf_op jit(solution)/shard_map/while
  742.6 6.0 copy-start.36
  742.6 7.3 copy-start.37
  742.7 8.6 copy-start.38
  744.4 9.2 copy-start.12
  745.1 8.5 copy-start.24
  748.6 5.2 copy-start.25
  764.0 11.1 %copy-start.29 = (bf16[11,256]{1,0:T(8,128)(2,1)S(1)}, bf16[11,256]{1,0:T(8,128)(2,1)}, u32[]{:S(2)}) copy-start(bf16[11,256]{1,0:T(8,128)(2,1)} %get-tuple-element.2475) | copy-start | bytes 16900 | tf_op jit(solution)/shard_map/while
  777.6 4.1 copy-start.26
  798.5 6.0 copy-start.2
  802.8 6.3 copy-start.1
  810.2 5.8 copy-start.3
  810.2 5.8 copy-start.5
  810.2 6.6 copy-start.8
  810.2 6.6 copy-start.16
  810.2 6.5 copy-start.18
  810.3 6.5 copy-start.20
  816.8 4.3 copy-start.17
  816.8 8.4 copy-start.19
  816.8 23.3 %copy-start.7 = (bf16[128,384]{1,0:T(8,128)(2,1)}, bf16[128,384]{1,0:T(8,128)(2,1)S(1)}, u32[]{:S(2)}) copy-start(bf16[128,384]{1,0:T(8,128)(2,1)S(1)} %get-tuple-element.2479) | copy-start | bytes 294916 | tf_op jit(solution)/shard_map/while
  819.5 20.9 %copy-start.6 = (bf16[4,128,128]{1,2,0:T(8,128)(2,1)}, bf16[4,128,128]{1,2,0:T(8,128)(2,1)S(1)}, u32[]{:S(2)}) copy-start(bf16[4,128,128]{1,2,0:T(8,128)(2,1)S(1)} %get-tuple-element.2280) | copy-start | bytes 393220 | tf_op jit(solution)/shard_map/while
  829.5 6.0 copy-start.36
  829.5 7.3 copy-start.37
  829.5 8.6 copy-start.38
  831.2 9.2 copy-start.12
  831.9 8.5 copy-start.24
  835.5 5.2 copy-start.25
  850.8 11.1 %copy-start.29 = (bf16[11,256]{1,0:T(8,128)(2,1)S(1)}, bf16[11,256]{1,0:T(8,128)(2,1)}, u32[]{:S(2)}) copy-start(bf16[11,256]{1,0:T(8,128)(2,1)} %get-tuple-element.2475) | copy-start | bytes 16900 | tf_op jit(solution)/shard_map/while
  864.5 4.1 copy-start.26
  885.4 6.0 copy-start.2
  889.7 6.3 copy-start.1
  897.1 5.9 copy-start.3
  897.1 5.9 copy-start.5
  897.1 6.6 copy-start.8
  897.1 6.6 copy-start.16
  897.1 6.6 copy-start.18
  897.1 6.6 copy-start.20
  905.6 9.1 all-to-all-start.3
  914.6 8.6 all-to-all-start.4
  (38 other events, 84.7 us)
where the time goes:
time: 938 us; the launch traced here: 924 us
  other arithmetic  498 us (53%)
  local copies, waits for them, and re-layouts  281 us (30%)
  matrix products  71.9 us (8%)
  starting transfers between devices  26.3 us (3%)
  waiting for transfers between devices  21.5 us (2%)
  loops' own time  16.9 us (2%)
    unnamed x25, other arithmetic  224 us
    gather x48, local copies, waits for them, and re-layouts, band_between(): jnp.take(profile, jnp.clip(differ + half_width, 0, 2 * half_width), axis=0)  217 us
    select_n x11, other arithmetic, band_between(): return jnp.where(inside, picked, jnp.zeros_like(picked))  161 us
    dot_general x24, matrix products, visit_step(): jnp.einsum('kys,st->kyt', current, middle_bands[profile_index], preferred...  25.5 us
    dot_general x24, matrix products, visit_step(): jnp.einsum('kyh,ht->kyt', head_cols, upper_bands[profile_index], preferre...  25.3 us
    reduce_sum x12, other arithmetic, visit_step(): picture = picture + jnp.sum(result * spatial, axis=2)  22.8 us
    concatenate x6, other arithmetic, per_device(): jnp.concatenate([band_between(profiles[horizontal_list[basis]], col_axis,...  21.8 us
  transfers between devices with their start and end apart: 5, of which 3 were waited for; matrix products, arithmetic and copies ran while one was open for 73% of the time, Pallas kernels for 0%

commit v1 on v0

v1 whole, which is shorter than its diff:
```python
import functools

import jax
import jax.numpy as jnp
import ml_dtypes
import numpy as np
from jax import lax
from jax.experimental import pallas as pl
from jax.experimental.pallas import tpu as pltpu
from jax.sharding import PartitionSpec as P

TAPS = 23
HALF = 11
SPREADS = (0.7, 1.5, 3.0)
DEGREES = (4, 3, 2)
MESH = pl.DeviceIdType.MESH
F32 = jnp.float32
BF16 = jnp.bfloat16


def profile_table():
    offsets = np.arange(-HALF, HALF + 1).astype(np.float64)
    profiles = []
    for spread, degree in zip(SPREADS, DEGREES):
        for power in range(degree + 1):
            profile = np.exp(-offsets * offsets / (2.0 * spread * spread)) * (offsets / spread) ** power
            profiles.append(profile / np.sqrt(np.sum(profile * profile)))
    return np.stack(profiles).astype(np.float32).astype(ml_dtypes.bfloat16).astype(np.float32)


def basis_pairs():
    pairs, start = [], 0
    for degree in DEGREES:
        for vertical in range(degree + 1):
            for horizontal in range(degree + 1 - vertical):
                pairs.append((start + vertical, start + horizontal))
        start += degree + 1
    return pairs


def band(profile, inputs, outputs):
    differ = outputs[None, :] - inputs[:, None]
    return np.where(np.abs(differ) <= HALF, profile[np.clip(differ + HALF, 0, 2 * HALF)], 0.0)


def tables(rows, width):
    profiles = profile_table()
    y = np.arange(rows)
    vertical = np.stack([band(p, y, y).T for p in profiles])
    x = np.arange(width)
    halo = np.where(x < width // 2, x + width, x - width)
    lanes = np.concatenate([x, halo])
    horizontal = np.concatenate([band(p, lanes, x) for p in profiles], axis=1)
    return vertical.astype(np.float32), horizontal.astype(ml_dtypes.bfloat16)


def kernel(
    groups, patches,
    patch_ref, slot_ref, coef_ref, img_hbm, wgt_hbm, ver_hbm, hor_hbm, out_ref,
    img_in, wgt_in, ver, band_h, img_send, img_recv, wgt_send, wgt_recv, lab_send, lab_recv,
    win, hor, mix, mat, mat_send, mat_recv,
    in_sem, lab_ssem, lab_rsem, fwd_ssem, fwd_rsem, img_ssem, img_rsem,
    wgt_ssem, wgt_osem, wgt_rsem, mat_ssem, mat_rsem,
):
    my_group, me = lax.axis_index("group"), lax.axis_index("patch")
    strips, rows, width = img_in.shape
    visits, cols = mat.shape[0], mat.shape[2]
    blocks = strips // visits
    slab = rows // groups
    count = ver.shape[0]
    devices = groups * patches

    loads = [
        pltpu.make_async_copy(src, dst, in_sem.at[i])
        for i, (src, dst) in enumerate(
            [(img_hbm.at[0], img_in), (wgt_hbm.at[0], wgt_in), (ver_hbm, ver), (hor_hbm, band_h)]
        )
    ]
    for load in loads:
        load.start()

    barrier = pltpu.get_barrier_semaphore()
    mine = my_group * patches + me

    def greet(i, carry):
        other = lax.rem(mine + 1 + i, devices)
        pl.semaphore_signal(
            barrier, inc=1, device_id=(other // patches, lax.rem(other, patches)), device_id_type=MESH
        )
        return carry

    lax.fori_loop(0, devices - 1, greet, 0)

    def source_of(p):
        source, label = jnp.int32(0), jnp.int32(0)
        for s in range(strips):
            here = patch_ref[0, s] == p
            source = jnp.where(here, s, source)
            label = jnp.where(here, slot_ref[0, s] + 1, label)
        return source, label

    def pack_label(p, carry):
        _, label = source_of(p)
        lab_send[p] = jnp.full((1, 128), label, jnp.int32)
        return carry

    def pack_image(p, carry):
        source, _ = source_of(p)
        img_send[p] = img_in[source]
        return carry

    def pack_weight(p, carry):
        source, _ = source_of(p)
        wgt_send[p] = wgt_in[source]
        return carry

    def other_patch(i):
        return lax.rem(me + 1 + lax.rem(i + patches // 4, patches - 1), patches)

    lax.fori_loop(0, patches, pack_label, 0)
    loads[0].wait()
    lax.fori_loop(0, patches, pack_image, 0)
    pl.semaphore_wait(barrier, devices - 1)

    def send_label(i, carry):
        p = other_patch(i)
        pltpu.make_async_remote_copy(
            src_ref=lab_send.at[p], dst_ref=lab_recv.at[my_group, me],
            send_sem=lab_ssem, recv_sem=lab_rsem, device_id=(my_group, p), device_id_type=MESH,
        ).start()
        return carry

    def send_image(i, carry):
        p = other_patch(i)
        pltpu.make_async_remote_copy(
            src_ref=img_send.at[p], dst_ref=img_recv.at[me],
            send_sem=img_ssem, recv_sem=img_rsem, device_id=(my_group, p), device_id_type=MESH,
        ).start()
        return carry

    lax.fori_loop(0, patches - 1, send_label, 0)
    pltpu.make_async_copy(lab_send.at[me], lab_recv.at[my_group, me], lab_rsem).start()
    lax.fori_loop(0, patches - 1, send_image, 0)
    pltpu.make_async_copy(img_send.at[me], img_recv.at[me], img_rsem).start()

    loads[1].wait()
    lax.fori_loop(0, patches, pack_weight, 0)

    loads[2].wait()
    pairs = basis_pairs()
    down = (2.0 * lax.broadcasted_iota(jnp.int32, (rows, rows), 0).astype(F32) - (rows - 1)) / (rows - 1)

    def mix_visit(v, carry):
        for r in range(count):
            flat = jnp.zeros((rows, rows), F32)
            across = jnp.zeros((rows, rows), F32)
            tilt = jnp.zeros((rows, rows), F32)
            for b, (q, h) in enumerate(pairs):
                if h == r:
                    vertical = ver[q]
                    flat = flat + coef_ref[v, 0, b] * vertical
                    across = across + coef_ref[v, 1, b] * vertical
                    tilt = tilt + coef_ref[v, 2, b] * vertical
            mix[v, :rows, r * rows : (r + 1) * rows] = (flat + down * tilt).astype(BF16)
            mix[v, rows:, r * rows : (r + 1) * rows] = across.astype(BF16)
        return carry

    lax.fori_loop(0, visits, mix_visit, 0)

    pltpu.make_async_copy(img_send.at[pl.ds(0, patches - 1)], img_send.at[pl.ds(0, patches - 1)], img_ssem).wait()

    def slab_of(g):
        return pl.ds(pl.multiple_of(g * slab, slab), slab)

    for d in range(groups):
        g = lax.rem(my_group + d, groups)

        def send_weight(i, carry, d=d, g=g):
            p = other_patch(i)
            pltpu.make_async_remote_copy(
                src_ref=wgt_send.at[p, slab_of(g)], dst_ref=wgt_recv.at[my_group, me],
                send_sem=wgt_osem if d == 0 else wgt_ssem, recv_sem=wgt_rsem,
                device_id=(g, p), device_id_type=MESH,
            ).start()
            return carry

        lax.fori_loop(0, patches - 1, send_weight, 0)
        if d == 0:
            pltpu.make_async_copy(wgt_send.at[me, slab_of(g)], wgt_recv.at[my_group, me], wgt_rsem).start()
        else:
            pltpu.make_async_remote_copy(
                src_ref=wgt_send.at[me, slab_of(g)], dst_ref=wgt_recv.at[my_group, me],
                send_sem=wgt_ssem, recv_sem=wgt_rsem, device_id=(g, me), device_id_type=MESH,
            ).start()

    pltpu.make_async_copy(lab_recv.at[0], lab_recv.at[0], lab_rsem).wait()
    for d in range(1, groups):
        pltpu.make_async_remote_copy(
            src_ref=lab_recv.at[my_group], dst_ref=lab_recv.at[my_group],
            send_sem=fwd_ssem, recv_sem=fwd_rsem,
            device_id=(lax.rem(my_group + d, groups), me), device_id_type=MESH,
        ).start()

    def positions(g):
        labels = lab_recv[g]
        order = lax.broadcasted_iota(jnp.int32, labels.shape, 0)
        return [
            jnp.max(jnp.where(labels == t + 1, order, 0)) for t in range(strips)
        ]

    place = positions(my_group)
    pltpu.make_async_copy(img_recv, img_recv, img_rsem).wait()

    zeros = jnp.zeros((rows, width), BF16)
    half = width // 2
    for t in range(strips):
        k = t % blocks
        here = slice(t * rows, (t + 1) * rows)
        win[here, :width] = img_recv[place[t]]
        right = img_recv[place[t + 1]] if k < blocks - 1 else zeros
        left = img_recv[place[t - 1]] if k > 0 else zeros
        win[here, width : width + half] = right[:, :half]
        win[here, width + half :] = left[:, half:]

    loads[3].wait()
    per = 2
    for v in range(visits):
        for j in range(count // per):
            part = jnp.dot(
                win[v * blocks * rows : (v + 1) * blocks * rows, :],
                band_h[:, j * per * width : (j + 1) * per * width],
                preferred_element_type=F32,
            ).astype(BF16)
            for k in range(blocks):
                for i in range(per):
                    r = j * per + i
                    hor[v, r * rows : (r + 1) * rows, k * width : (k + 1) * width] = part[
                        k * rows : (k + 1) * rows, i * width : (i + 1) * width
                    ]

    chunk = 2 * width
    for v in range(visits):
        for c in range(cols // chunk):
            here = slice(c * chunk, (c + 1) * chunk)
            both = jnp.dot(mix[v], hor[v, :, here], preferred_element_type=F32)
            at = lax.broadcasted_iota(jnp.int32, (rows, chunk), 1).astype(F32) + c * chunk
            sideways = (2.0 * at - (cols - 1)) / (cols - 1)
            matched = both[:rows] + sideways * both[rows:]
            mat[v, :, here] = matched
            mat_send[v, :, here] = matched.astype(BF16)
        for d in range(1, groups):
            g = lax.rem(my_group + d, groups)
            pltpu.make_async_remote_copy(
                src_ref=mat_send.at[v, slab_of(g)], dst_ref=mat_recv.at[my_group, v],
                send_sem=mat_ssem, recv_sem=mat_rsem, device_id=(g, me), device_id_type=MESH,
            ).start()

    rest = pl.ds(0, groups - 1)
    pltpu.make_async_copy(lab_recv.at[rest], lab_recv.at[rest], fwd_rsem).wait()
    places = [place]
    for d in range(1, groups):
        places.append(positions(lax.rem(my_group + d, groups)))
    pltpu.make_async_copy(mat_recv.at[rest], mat_recv.at[rest], mat_rsem).wait()
    pltpu.make_async_copy(wgt_recv, wgt_recv, wgt_rsem).wait()

    for k in range(blocks):
        here = slice(k * width, (k + 1) * width)
        numer = jnp.zeros((slab, width), F32)
        denom = jnp.zeros((slab, width), F32)
        for d in range(groups):
            g = lax.rem(my_group + d, groups)
            for v in range(visits):
                weight = wgt_recv[g, places[d][v * blocks + k]].astype(F32)
                if d == 0:
                    matched = mat[v, slab_of(my_group), here]
                else:
                    matched = mat_recv[g, v, :, here].astype(F32)
                numer = numer + weight * matched
                denom = denom + weight
        out_ref[0, :, here] = numer / denom

    some = pl.ds(0, patches - 1)
    pltpu.make_async_copy(lab_send.at[some], lab_send.at[some], lab_ssem).wait()
    pltpu.make_async_copy(lab_recv.at[rest], lab_recv.at[rest], fwd_ssem).wait()
    pltpu.make_async_copy(wgt_recv.at[0, some], wgt_recv.at[0, some], wgt_osem).wait()
    pltpu.make_async_copy(wgt_recv.at[rest], wgt_recv.at[rest], wgt_ssem).wait()
    pltpu.make_async_copy(mat_recv.at[rest], mat_recv.at[rest], mat_ssem).wait()


def solution(mesh):
    groups, patches = mesh.shape["group"], mesh.shape["patch"]

    def per_device(strip_image, strip_weight, strip_patch, strip_slot, kernel_coef):
        _, strips, rows, width = strip_image.shape
        visits = kernel_coef.shape[2]
        cols = strips // visits * width
        slab = rows // groups
        vertical, horizontal = tables(rows, width)
        count = vertical.shape[0]
        smem = pl.BlockSpec(memory_space=pltpu.SMEM)
        anywhere = pl.BlockSpec(memory_space=pl.ANY)
        dma = pltpu.SemaphoreType.DMA
        macs = visits * cols * rows * count * (2 * width + 2 * rows)
        return pl.pallas_call(
            functools.partial(kernel, groups, patches),
            out_shape=jax.ShapeDtypeStruct((1, slab, cols), F32),
            in_specs=[smem, smem, smem, anywhere, anywhere, anywhere, anywhere],
            out_specs=pl.BlockSpec(memory_space=pltpu.VMEM),
            scratch_shapes=[
                pltpu.VMEM((strips, rows, width), BF16),
                pltpu.VMEM((strips, rows, width), BF16),
                pltpu.VMEM(vertical.shape, F32),
                pltpu.VMEM(horizontal.shape, BF16),
                pltpu.VMEM((patches, rows, width), BF16),
                pltpu.VMEM((patches, rows, width), BF16),
                pltpu.VMEM((patches, rows, width), BF16),
                pltpu.VMEM((groups, patches, slab, width), BF16),
                pltpu.VMEM((patches, 1, 128), jnp.int32),
                pltpu.VMEM((groups, patches, 1, 128), jnp.int32),
                pltpu.VMEM((strips * rows, 2 * width), BF16),
                pltpu.VMEM((visits, count * rows, cols), BF16),
                pltpu.VMEM((visits, 2 * rows, count * rows), BF16),
                pltpu.VMEM((visits, rows, cols), F32),
                pltpu.VMEM((visits, rows, cols), BF16),
                pltpu.VMEM((groups, visits, slab, cols), BF16),
                dma((4,)),
            ]
            + [dma] * 11,
            compiler_params=pltpu.CompilerParams(
                collective_id=0, has_side_effects=True, vmem_limit_bytes=40 * 1024 * 1024
            ),
            cost_estimate=pl.CostEstimate(flops=2 * macs, bytes_accessed=1 << 21, transcendentals=0),
        )(
            strip_patch, strip_slot, kernel_coef[0, 0], strip_image, strip_weight,
            jnp.asarray(vertical), jnp.asarray(horizontal),
        )

    return jax.shard_map(
        per_device,
        mesh=mesh,
        in_specs=(
            P("group", "patch", None, None),
            P("group", "patch", None, None),
            P("group", "patch"),
            P("group", "patch"),
            P("group", "patch", None, None, None),
        ),
        out_specs=P("patch", "group", None),
        check_vma=False,
    )
```

time: 938 us -> 37.9 us (0.04); the launches traced: 924 us -> 37.4 us
  other arithmetic: 498 us -> 0 us
  local copies, waits for them, and re-layouts: 281 us -> 6.18 us
  matrix products: 71.9 us -> 0 us
  Pallas kernels: 0 us -> 31.2 us
  starting transfers between devices: 26.3 us -> 0 us
  waiting for transfers between devices: 21.5 us -> 0 us
  loops' own time: 16.9 us -> 0 us
    gather x71 -> x0, local copies, waits for them, and re-layouts: 231 us -> none  [the longest x48 217 us: band_between(): jnp.take(profile, jnp.clip(differ + half_width, 0, 2 * half_width), axis=0)]
    unnamed x25 -> x0, other arithmetic: 224 us -> none
    select_n x16 -> x0, other arithmetic: 163 us -> none  [the longest x11 161 us: band_between(): return jnp.where(inside, picked, jnp.zeros_like(picked))]
    dot_general x74 -> x0, matrix products: 71.9 us -> none  [the longest x24 25.5 us: visit_step(): jnp.einsum('kys,st->kyt', current, middle_bands[profile_index], preferred...]
    concatenate x24 -> x0, other arithmetic: 41.7 us -> none  [the longest x6 21.8 us: per_device(): jnp.concatenate([band_between(profiles[horizontal_list[basis]], col_axis,...]
    reduce_sum x29 -> x0, other arithmetic: 32 us -> none  [the longest x12 22.8 us: visit_step(): picture = picture + jnp.sum(result * spatial, axis=2)]
    pallas_call x0 -> x1, Pallas kernels: none -> 31.2 us  [per_device(): pl.pallas_call(functools.partial(kernel, groups, patches), out_shape=jax....]
    all_to_all x5 -> x0, starting transfers between devices: 26.3 us -> none  [the longest x1 7.36 us: per_device(): lax.all_to_all(send_label, 'patch', split_axis=0, concat_axis=0, tiled=True)]
  transfers between devices with their start and end apart: 5 -> 0, of which waited for: 3 -> 0; matrix products, arithmetic and copies ran while one was open for 73% -> 0% of each run, Pallas kernels for 0% -> 0%
where the time goes in v1:
time: 37.9 us; the launch traced here: 37.4 us
  Pallas kernels  31.2 us (82%)
  local copies, waits for them, and re-layouts  6.18 us (16%)
    pallas_call x1, Pallas kernels, per_device(): pl.pallas_call(functools.partial(kernel, groups, patches), out_shape=jax....  31.2 us
    unnamed x14, local copies, waits for them, and re-layouts  6.18 us

profile of v1, /device:TPU:0, one launch (start us, length us, event | category | flops | bytes accessed | tf_op | source)
XLA Modules:
  0.0 37.4 jit_solution(14422534098994902786)
XLA Ops:
  0.0 0.7 %copy.10 = f32[1,1,2,3,31]{4,3,2,1,0:T(4,128)S(1)} copy(f32[1,1,2,3,31]{4,2,3,1,0:T(2,128)} %param.11) | data formatting | bytes 1488 | tf_op args[4]
  0.7 0.0 copy-start.2
  0.7 0.0 copy-start.3
  0.7 0.7 %copy-done.2 = s32[1,8]{1,0:T(1,128)S(1)} copy-done((s32[1,8]{1,0:T(1,128)S(1)}, s32[1,8]{1,0:T(1,128)}, u32[]{:S(2)}) %copy-start.2) | copy-done | bytes 56
  1.3 0.0 copy-done.3
  1.4 0.0 copy-start
  1.4 0.9 %copy-done = bf16[1,8,128,128]{3,2,1,0:T(8,128)(2,1)S(1)} copy-done((bf16[1,8,128,128]{3,2,1,0:T(8,128)(2,1)S(1)}, bf16[1,8,128,128]{3,2,1,0:T(8,128)(2,1)}, u32[]{:S(2)}) %copy-start) | copy-done | bytes 262168
  2.3 0.0 copy-start.1
  2.3 0.9 %copy-done.1 = bf16[1,8,128,128]{3,2,1,0:T(8,128)(2,1)S(1)} copy-done((bf16[1,8,128,128]{3,2,1,0:T(8,128)(2,1)S(1)}, bf16[1,8,128,128]{3,2,1,0:T(8,128)(2,1)}, u32[]{:S(2)}) %copy-start.1) | copy-done | bytes 262168
  3.3 0.0 copy-start.4
  3.3 1.1 %copy-done.4 = bf16[256,1536]{1,0:T(8,128)(2,1)S(1)} copy-done((bf16[256,1536]{1,0:T(8,128)(2,1)S(1)}, bf16[256,1536]{1,0:T(8,128)(2,1)}, u32[]{:S(2)}) %copy-start.4) | copy-done | bytes 786456
  4.4 0.0 copy-start.5
  4.4 1.1 %copy-done.5 = f32[12,128,128]{2,1,0:T(8,128)S(1)} copy-done((f32[12,128,128]{2,1,0:T(8,128)S(1)}, f32[12,128,128]{2,1,0:T(8,128)}, u32[]{:S(2)}) %copy-start.5) | copy-done | bytes 786456
  5.5 31.2 %shard_map.73 = f32[1,64,512]{2,1,0:T(8,128)S(1)} custom-call(s32[1,8]{1,0:T(1,128)S(1)} %copy-done.2, s32[1,8]{1,0:T(1,128)S(1)} %copy-done.3, f32[2,3,31]{2,1,0:T(4,128)S(1)} %bitcast.3, bf16[1,8,128,128]{3,2,1,0:T(8,128)(2,1)S(1)} %copy-done, bf16[1,8,128,128]{3,2,1,0:T(8,128)(2,1)S(1)} %copy-done.1, f32[12,128,128]{2,1,0:T(8,128)S(1)} %copy-done.5, ...), custom_call_target="tpu_custom_call" | custom-call | flops 1610612736 | bytes 2097152 | tf_op jit(solution)/shard_map/pallas_call | solution.py:304
  36.8 0.7 %copy.12 = f32[1,64,512]{2,1,0:T(8,128)} copy(f32[1,64,512]{2,1,0:T(8,128)S(1)} %shard_map.73) | data formatting | bytes 262144
Async XLA Ops:
  0.7 0.7 %copy-start.2 = (s32[1,8]{1,0:T(1,128)S(1)}, s32[1,8]{1,0:T(1,128)}, u32[]{:S(2)}) copy-start(s32[1,8]{1,0:T(1,128)} %patch_ref.1) | copy-start | bytes 100
  0.7 0.7 %copy-start.3 = (s32[1,8]{1,0:T(1,128)S(1)}, s32[1,8]{1,0:T(1,128)}, u32[]{:S(2)}) copy-start(s32[1,8]{1,0:T(1,128)} %slot_ref.1) | copy-start | bytes 100
  1.4 0.9 %copy-start = (bf16[1,8,128,128]{3,2,1,0:T(8,128)(2,1)S(1)}, bf16[1,8,128,128]{3,2,1,0:T(8,128)(2,1)}, u32[]{:S(2)}) copy-start(bf16[1,8,128,128]{3,2,1,0:T(8,128)(2,1)} %img_hbm.1) | copy-start | bytes 786436
  2.3 0.9 %copy-start.1 = (bf16[1,8,128,128]{3,2,1,0:T(8,128)(2,1)S(1)}, bf16[1,8,128,128]{3,2,1,0:T(8,128)(2,1)}, u32[]{:S(2)}) copy-start(bf16[1,8,128,128]{3,2,1,0:T(8,128)(2,1)} %wgt_hbm.1) | copy-start | bytes 786436
  3.3 1.1 %copy-start.4 = (bf16[256,1536]{1,0:T(8,128)(2,1)S(1)}, bf16[256,1536]{1,0:T(8,128)(2,1)}, u32[]{:S(2)}) copy-start(bf16[256,1536]{1,0:T(8,128)(2,1)} %constant.5.clone.hor_hbm) | copy-start | bytes 2359300
  4.4 1.1 %copy-start.5 = (f32[12,128,128]{2,1,0:T(8,128)S(1)}, f32[12,128,128]{2,1,0:T(8,128)}, u32[]{:S(2)}) copy-start(f32[12,128,128]{2,1,0:T(8,128)} %constant.4.clone.ver_hbm) | copy-start | bytes 2359300

commit v2 on v1

--- a/solution.py
+++ b/solution.py
@@ -56,7 +56,8 @@
 
 def kernel(
     groups, patches,
-    patch_ref, slot_ref, coef_ref, img_hbm, wgt_hbm, ver_hbm, hor_hbm, out_ref,
+    patch_hbm, slot_hbm, coef_hbm, img_hbm, wgt_hbm, ver_hbm, hor_hbm, out_ref,
+    patch_ref, slot_ref, coef_ref,
     img_in, wgt_in, ver, band_h, img_send, img_recv, wgt_send, wgt_recv, lab_send, lab_recv,
     win, hor, mix, mat, mat_send, mat_recv,
     in_sem, lab_ssem, lab_rsem, fwd_ssem, fwd_rsem, img_ssem, img_rsem,
@@ -73,11 +74,14 @@
     loads = [
         pltpu.make_async_copy(src, dst, in_sem.at[i])
         for i, (src, dst) in enumerate(
-            [(img_hbm.at[0], img_in), (wgt_hbm.at[0], wgt_in), (ver_hbm, ver), (hor_hbm, band_h)]
+            [
+                (img_hbm.at[0], img_in), (wgt_hbm.at[0], wgt_in), (ver_hbm, ver), (hor_hbm, band_h),
+                (patch_hbm, patch_ref), (slot_hbm, slot_ref), (coef_hbm, coef_ref),
+            ]
         )
     ]
-    for load in loads:
-        load.start()
+    for i in (4, 5, 0, 1, 6, 2, 3):
+        loads[i].start()
 
     barrier = pltpu.get_barrier_semaphore()
     mine = my_group * patches + me
@@ -117,6 +121,8 @@
     def other_patch(i):
         return lax.rem(me + 1 + lax.rem(i + patches // 4, patches - 1), patches)
 
+    loads[4].wait()
+    loads[5].wait()
     lax.fori_loop(0, patches, pack_label, 0)
     loads[0].wait()
     lax.fori_loop(0, patches, pack_image, 0)
@@ -147,6 +153,7 @@
     lax.fori_loop(0, patches, pack_weight, 0)
 
     loads[2].wait()
+    loads[6].wait()
     pairs = basis_pairs()
     down = (2.0 * lax.broadcasted_iota(jnp.int32, (rows, rows), 0).astype(F32) - (rows - 1)) / (rows - 1)
 
@@ -158,9 +165,9 @@
             for b, (q, h) in enumerate(pairs):
                 if h == r:
                     vertical = ver[q]
-                    flat = flat + coef_ref[v, 0, b] * vertical
-                    across = across + coef_ref[v, 1, b] * vertical
-                    tilt = tilt + coef_ref[v, 2, b] * vertical
+                    flat = flat + coef_ref[0, v, b] * vertical
+                    across = across + coef_ref[1, v, b] * vertical
+                    tilt = tilt + coef_ref[2, v, b] * vertical
             mix[v, :rows, r * rows : (r + 1) * rows] = (flat + down * tilt).astype(BF16)
             mix[v, rows:, r * rows : (r + 1) * rows] = across.astype(BF16)
         return carry
@@ -297,16 +304,19 @@
         slab = rows // groups
         vertical, horizontal = tables(rows, width)
         count = vertical.shape[0]
-        smem = pl.BlockSpec(memory_space=pltpu.SMEM)
-        anywhere = pl.BlockSpec(memory_space=pl.ANY)
+        far = pl.BlockSpec(memory_space=pltpu.HBM)
+        coef = jnp.transpose(kernel_coef[0, 0], (1, 0, 2))
         dma = pltpu.SemaphoreType.DMA
         macs = visits * cols * rows * count * (2 * width + 2 * rows)
         return pl.pallas_call(
             functools.partial(kernel, groups, patches),
             out_shape=jax.ShapeDtypeStruct((1, slab, cols), F32),
-            in_specs=[smem, smem, smem, anywhere, anywhere, anywhere, anywhere],
+            in_specs=[far] * 7,
             out_specs=pl.BlockSpec(memory_space=pltpu.VMEM),
             scratch_shapes=[
+                pltpu.SMEM(strip_patch.shape, jnp.int32),
+                pltpu.SMEM(strip_slot.shape, jnp.int32),
+                pltpu.SMEM(coef.shape, F32),
                 pltpu.VMEM((strips, rows, width), BF16),
                 pltpu.VMEM((strips, rows, width), BF16),
                 pltpu.VMEM(vertical.shape, F32),
@@ -323,15 +333,15 @@
                 pltpu.VMEM((visits, rows, cols), F32),
                 pltpu.VMEM((visits, rows, cols), BF16),
                 pltpu.VMEM((groups, visits, slab, cols), BF16),
-                dma((4,)),
+                dma((7,)),
             ]
             + [dma] * 11,
             compiler_params=pltpu.CompilerParams(
-                collective_id=0, has_side_effects=True, vmem_limit_bytes=40 * 1024 * 1024
+                collective_id=0, has_side_effects=True, vmem_limit_bytes=64 * 1024 * 1024
             ),
             cost_estimate=pl.CostEstimate(flops=2 * macs, bytes_accessed=1 << 21, transcendentals=0),
         )(
-            strip_patch, strip_slot, kernel_coef[0, 0], strip_image, strip_weight,
+            strip_patch, strip_slot, coef, strip_image, strip_weight,
             jnp.asarray(vertical), jnp.asarray(horizontal),
         )
 

time: 37.9 us -> 33 us (0.87)
  local copies, waits for them, and re-layouts: 6.18 us -> 1.57 us
    unnamed x14 -> x1, local copies, waits for them, and re-layouts: 6.18 us -> 1.57 us
where the time goes in v2:
time: 33 us; the launch traced here: 32.7 us
  Pallas kernels  31.1 us (94%)
  local copies, waits for them, and re-layouts  1.57 us (5%)
    pallas_call x1, Pallas kernels, per_device(): pl.pallas_call(functools.partial(kernel, groups, patches), out_shape=jax....  31.1 us
    unnamed x1, local copies, waits for them, and re-layouts  1.57 us

profile of v2, /device:TPU:0, one launch (start us, length us, event | category | flops | bytes accessed | tf_op | source)
XLA Modules:
  0.0 32.7 jit_solution(12655031321157452172)
XLA Ops:
  0.0 31.1 %shard_map.73 = f32[1,64,512]{2,1,0:T(8,128)} custom-call(s32[1,8]{1,0:T(1,128)} %patch_hbm.1, s32[1,8]{1,0:T(1,128)} %slot_hbm.1, f32[3,2,31]{2,1,0:T(2,128)} %bitcast.3, bf16[1,8,128,128]{3,2,1,0:T(8,128)(2,1)} %img_hbm.1, bf16[1,8,128,128]{3,2,1,0:T(8,128)(2,1)} %wgt_hbm.1, f32[12,128,128]{2,1,0:T(8,128)} %constant.4.clone.ver_hbm, ...), custom_call_target="tpu_custom_call" | custom-call | flops 1610612736 | bytes 2097152 | tf_op jit(solution)/shard_map/pallas_call | solution.py:311
  31.1 1.6 %copy.9 = f32[1,64,512]{2,1,0:T(8,128)} copy(f32[1,64,512]{2,1,0:T(8,128)} %shard_map.73) | data formatting | bytes 262144

commit v3 on v2

--- a/solution.py
+++ b/solution.py
@@ -152,6 +152,30 @@
     loads[1].wait()
     lax.fori_loop(0, patches, pack_weight, 0)
 
+    def slab_of(g):
+        return pl.ds(pl.multiple_of(g * slab, slab), slab)
+
+    for d in range(groups):
+        g = lax.rem(my_group + d, groups)
+
+        def send_weight(i, carry, d=d, g=g):
+            p = other_patch(i)
+            pltpu.make_async_remote_copy(
+                src_ref=wgt_send.at[p, slab_of(g)], dst_ref=wgt_recv.at[my_group, me],
+                send_sem=wgt_osem if d == 0 else wgt_ssem, recv_sem=wgt_rsem,
+                device_id=(g, p), device_id_type=MESH,
+            ).start()
+            return carry
+
+        lax.fori_loop(0, patches - 1, send_weight, 0)
+        if d == 0:
+            pltpu.make_async_copy(wgt_send.at[me, slab_of(g)], wgt_recv.at[my_group, me], wgt_rsem).start()
+        else:
+            pltpu.make_async_remote_copy(
+                src_ref=wgt_send.at[me, slab_of(g)], dst_ref=wgt_recv.at[my_group, me],
+                send_sem=wgt_ssem, recv_sem=wgt_rsem, device_id=(g, me), device_id_type=MESH,
+            ).start()
+
     loads[2].wait()
     loads[6].wait()
     pairs = basis_pairs()
@@ -173,32 +197,6 @@
         return carry
 
     lax.fori_loop(0, visits, mix_visit, 0)
-
-    pltpu.make_async_copy(img_send.at[pl.ds(0, patches - 1)], img_send.at[pl.ds(0, patches - 1)], img_ssem).wait()
-
-    def slab_of(g):
-        return pl.ds(pl.multiple_of(g * slab, slab), slab)
-
-    for d in range(groups):
-        g = lax.rem(my_group + d, groups)
-
-        def send_weight(i, carry, d=d, g=g):
-            p = other_patch(i)
-            pltpu.make_async_remote_copy(
-                src_ref=wgt_send.at[p, slab_of(g)], dst_ref=wgt_recv.at[my_group, me],
-                send_sem=wgt_osem if d == 0 else wgt_ssem, recv_sem=wgt_rsem,
-                device_id=(g, p), device_id_type=MESH,
-            ).start()
-            return carry
-
-        lax.fori_loop(0, patches - 1, send_weight, 0)
-        if d == 0:
-            pltpu.make_async_copy(wgt_send.at[me, slab_of(g)], wgt_recv.at[my_group, me], wgt_rsem).start()
-        else:
-            pltpu.make_async_remote_copy(
-                src_ref=wgt_send.at[me, slab_of(g)], dst_ref=wgt_recv.at[my_group, me],
-                send_sem=wgt_ssem, recv_sem=wgt_rsem, device_id=(g, me), device_id_type=MESH,
-            ).start()
 
     pltpu.make_async_copy(lab_recv.at[0], lab_recv.at[0], lab_rsem).wait()
     for d in range(1, groups):
@@ -287,6 +285,7 @@
         out_ref[0, :, here] = numer / denom
 
     some = pl.ds(0, patches - 1)
+    pltpu.make_async_copy(img_send.at[some], img_send.at[some], img_ssem).wait()
     pltpu.make_async_copy(lab_send.at[some], lab_send.at[some], lab_ssem).wait()
     pltpu.make_async_copy(lab_recv.at[rest], lab_recv.at[rest], fwd_ssem).wait()
     pltpu.make_async_copy(wgt_recv.at[0, some], wgt_recv.at[0, some], wgt_osem).wait()

time: 33 us -> 33.1 us (level)
  the two profiles are of different devices: /device:TPU:0 before, /device:TPU:11 now
where the time goes in v3:
time: 33.1 us; the launch traced here: 32.9 us
  Pallas kernels  31.4 us (95%)
  local copies, waits for them, and re-layouts  1.57 us (5%)
    pallas_call x1, Pallas kernels, per_device(): pl.pallas_call(functools.partial(kernel, groups, patches), out_shape=jax....  31.4 us
    unnamed x1, local copies, waits for them, and re-layouts  1.57 us

profile of v3, /device:TPU:11, one launch (start us, length us, event | category | flops | bytes accessed | tf_op | source)
XLA Modules:
  0.0 32.9 jit_solution(8312603485684214410)
XLA Ops:
  0.0 31.4 %shard_map.73 = f32[1,64,512]{2,1,0:T(8,128)} custom-call(s32[1,8]{1,0:T(1,128)} %patch_hbm.1, s32[1,8]{1,0:T(1,128)} %slot_hbm.1, f32[3,2,31]{2,1,0:T(2,128)} %bitcast.3, bf16[1,8,128,128]{3,2,1,0:T(8,128)(2,1)} %img_hbm.1, bf16[1,8,128,128]{3,2,1,0:T(8,128)(2,1)} %wgt_hbm.1, f32[12,128,128]{2,1,0:T(8,128)} %constant.4.clone.ver_hbm, ...), custom_call_target="tpu_custom_call" | custom-call | flops 1610612736 | bytes 2097152 | tf_op jit(solution)/shard_map/pallas_call | solution.py:310
  31.4 1.6 %copy.9 = f32[1,64,512]{2,1,0:T(8,128)} copy(f32[1,64,512]{2,1,0:T(8,128)} %shard_map.73) | data formatting | bytes 262144

commit v4 on v2

--- a/solution.py
+++ b/solution.py
@@ -60,7 +60,7 @@
     patch_ref, slot_ref, coef_ref,
     img_in, wgt_in, ver, band_h, img_send, img_recv, wgt_send, wgt_recv, lab_send, lab_recv,
     win, hor, mix, mat, mat_send, mat_recv,
-    in_sem, lab_ssem, lab_rsem, fwd_ssem, fwd_rsem, img_ssem, img_rsem,
+    in_sem, lab_ssem, lab_rsem, fwd_ssem, fwd_rsem, img_fsem, img_ssem, img_rsem,
     wgt_ssem, wgt_osem, wgt_rsem, mat_ssem, mat_rsem,
 ):
     my_group, me = lax.axis_index("group"), lax.axis_index("patch")
@@ -119,7 +119,12 @@
         return carry
 
     def other_patch(i):
-        return lax.rem(me + 1 + lax.rem(i + patches // 4, patches - 1), patches)
+        step = lax.select(lax.rem(i, 2) == 0, patches // 2 + lax.div(i, 2), lax.div(i + 1, 2))
+        other, bit = jnp.int32(0), 1
+        while bit < patches:
+            other = other + bit * lax.rem(lax.div(me, bit) + lax.div(step, bit), 2)
+            bit *= 2
+        return other
 
     loads[4].wait()
     loads[5].wait()
@@ -136,17 +141,19 @@
         ).start()
         return carry
 
-    def send_image(i, carry):
+    def send_image(i, carry, sem=img_ssem):
         p = other_patch(i)
         pltpu.make_async_remote_copy(
             src_ref=img_send.at[p], dst_ref=img_recv.at[me],
-            send_sem=img_ssem, recv_sem=img_rsem, device_id=(my_group, p), device_id_type=MESH,
+            send_sem=sem, recv_sem=img_rsem, device_id=(my_group, p), device_id_type=MESH,
         ).start()
         return carry
 
+    first = patches // 2
+    lax.fori_loop(0, first, functools.partial(send_image, sem=img_fsem), 0)
     lax.fori_loop(0, patches - 1, send_label, 0)
     pltpu.make_async_copy(lab_send.at[me], lab_recv.at[my_group, me], lab_rsem).start()
-    lax.fori_loop(0, patches - 1, send_image, 0)
+    lax.fori_loop(first, patches - 1, send_image, 0)
     pltpu.make_async_copy(img_send.at[me], img_recv.at[me], img_rsem).start()
 
     loads[1].wait()
@@ -174,31 +181,30 @@
 
     lax.fori_loop(0, visits, mix_visit, 0)
 
-    pltpu.make_async_copy(img_send.at[pl.ds(0, patches - 1)], img_send.at[pl.ds(0, patches - 1)], img_ssem).wait()
+    pltpu.make_async_copy(img_send.at[pl.ds(0, first)], img_send.at[pl.ds(0, first)], img_fsem).wait()
 
     def slab_of(g):
         return pl.ds(pl.multiple_of(g * slab, slab), slab)
 
-    for d in range(groups):
-        g = lax.rem(my_group + d, groups)
-
-        def send_weight(i, carry, d=d, g=g):
-            p = other_patch(i)
+    def send_weight(i, carry):
+        p = other_patch(i)
+        for d in range(groups):
+            g = lax.rem(my_group + d, groups)
             pltpu.make_async_remote_copy(
                 src_ref=wgt_send.at[p, slab_of(g)], dst_ref=wgt_recv.at[my_group, me],
                 send_sem=wgt_osem if d == 0 else wgt_ssem, recv_sem=wgt_rsem,
                 device_id=(g, p), device_id_type=MESH,
             ).start()
-            return carry
-
-        lax.fori_loop(0, patches - 1, send_weight, 0)
-        if d == 0:
-            pltpu.make_async_copy(wgt_send.at[me, slab_of(g)], wgt_recv.at[my_group, me], wgt_rsem).start()
-        else:
-            pltpu.make_async_remote_copy(
-                src_ref=wgt_send.at[me, slab_of(g)], dst_ref=wgt_recv.at[my_group, me],
-                send_sem=wgt_ssem, recv_sem=wgt_rsem, device_id=(g, me), device_id_type=MESH,
-            ).start()
+        return carry
+
+    lax.fori_loop(0, patches - 1, send_weight, 0)
+    pltpu.make_async_copy(wgt_send.at[me, slab_of(my_group)], wgt_recv.at[my_group, me], wgt_rsem).start()
+    for d in range(1, groups):
+        g = lax.rem(my_group + d, groups)
+        pltpu.make_async_remote_copy(
+            src_ref=wgt_send.at[me, slab_of(g)], dst_ref=wgt_recv.at[my_group, me],
+            send_sem=wgt_ssem, recv_sem=wgt_rsem, device_id=(g, me), device_id_type=MESH,
+        ).start()
 
     pltpu.make_async_copy(lab_recv.at[0], lab_recv.at[0], lab_rsem).wait()
     for d in range(1, groups):
@@ -287,6 +293,8 @@
         out_ref[0, :, here] = numer / denom
 
     some = pl.ds(0, patches - 1)
+    last = pl.ds(0, patches - 1 - first)
+    pltpu.make_async_copy(img_send.at[last], img_send.at[last], img_ssem).wait()
     pltpu.make_async_copy(lab_send.at[some], lab_send.at[some], lab_ssem).wait()
     pltpu.make_async_copy(lab_recv.at[rest], lab_recv.at[rest], fwd_ssem).wait()
     pltpu.make_async_copy(wgt_recv.at[0, some], wgt_recv.at[0, some], wgt_osem).wait()
@@ -310,9 +318,10 @@
         macs = visits * cols * rows * count * (2 * width + 2 * rows)
         return pl.pallas_call(
             functools.partial(kernel, groups, patches),
-            out_shape=jax.ShapeDtypeStruct((1, slab, cols), F32),
+            out_shape=pltpu.VMEM((1, slab, cols), F32),
             in_specs=[far] * 7,
             out_specs=pl.BlockSpec(memory_space=pltpu.VMEM),
+
             scratch_shapes=[
                 pltpu.SMEM(strip_patch.shape, jnp.int32),
                 pltpu.SMEM(strip_slot.shape, jnp.int32),
@@ -335,14 +344,19 @@
                 pltpu.VMEM((groups, visits, slab, cols), BF16),
                 dma((7,)),
             ]
-            + [dma] * 11,
+            + [dma] * 12,
             compiler_params=pltpu.CompilerParams(
-                collective_id=0, has_side_effects=True, vmem_limit_bytes=64 * 1024 * 1024
+                collective_id=0, has_side_effects=True, vmem_limit_bytes=48 * 1024 * 1024
             ),
             cost_estimate=pl.CostEstimate(flops=2 * macs, bytes_accessed=1 << 21, transcendentals=0),
         )(
-            strip_patch, strip_slot, coef, strip_image, strip_weight,
-            jnp.asarray(vertical), jnp.asarray(horizontal),
+            *[
+                pltpu.with_memory_space_constraint(x, pltpu.HBM)
+                for x in (
+                    strip_patch, strip_slot, coef, strip_image, strip_weight,
+                    jnp.asarray(vertical), jnp.asarray(horizontal),
+                )
+            ]
         )
 
     return jax.shard_map(

time: 33 us -> 31.9 us (0.967)
  the two profiles are of different devices: /device:TPU:0 before, /device:TPU:9 now
where the time goes in v4:
time: 31.9 us; the launch traced here: 31.7 us
  Pallas kernels  31 us (97%)
  local copies, waits for them, and re-layouts  0.66 us (2%)
    pallas_call x1, Pallas kernels, per_device(): pl.pallas_call(functools.partial(kernel, groups, patches), out_shape=pltp...  31 us
    unnamed x1, local copies, waits for them, and re-layouts  0.66 us

profile of v4, /device:TPU:9, one launch (start us, length us, event | category | flops | bytes accessed | tf_op | source)
XLA Modules:
  0.0 31.7 jit_solution(6534912930186107190)
XLA Ops:
  0.0 31.0 %shard_map.73 = f32[1,64,512]{2,1,0:T(8,128)S(1)} custom-call(s32[1,8]{1,0:T(1,128)} %patch_hbm.1, s32[1,8]{1,0:T(1,128)} %slot_hbm.1, f32[3,2,31]{2,1,0:T(2,128)} %bitcast.3, bf16[1,8,128,128]{3,2,1,0:T(8,128)(2,1)} %img_hbm.1, bf16[1,8,128,128]{3,2,1,0:T(8,128)(2,1)} %wgt_hbm.1, f32[12,128,128]{2,1,0:T(8,128)} %constant.4.clone.ver_hbm, ...), custom_call_target="tpu_custom_call" | custom-call | flops 1610612736 | bytes 2097152 | tf_op jit(solution)/shard_map/pallas_call | solution.py:319
  31.0 0.7 %copy.9 = f32[1,64,512]{2,1,0:T(8,128)} copy(f32[1,64,512]{2,1,0:T(8,128)S(1)} %shard_map.73) | data formatting | bytes 262144

commit v5 on v4

--- a/solution.py
+++ b/solution.py
@@ -57,7 +57,7 @@
 def kernel(
     groups, patches,
     patch_hbm, slot_hbm, coef_hbm, img_hbm, wgt_hbm, ver_hbm, hor_hbm, out_ref,
-    patch_ref, slot_ref, coef_ref,
+    patch_ref, slot_ref, coef_ref, found,
     img_in, wgt_in, ver, band_h, img_send, img_recv, wgt_send, wgt_recv, lab_send, lab_recv,
     win, hor, mix, mat, mat_send, mat_recv,
     in_sem, lab_ssem, lab_rsem, fwd_ssem, fwd_rsem, img_fsem, img_ssem, img_rsem,
@@ -95,31 +95,30 @@
 
     lax.fori_loop(0, devices - 1, greet, 0)
 
-    def source_of(p):
+    def find(p, carry):
         source, label = jnp.int32(0), jnp.int32(0)
         for s in range(strips):
             here = patch_ref[0, s] == p
             source = jnp.where(here, s, source)
             label = jnp.where(here, slot_ref[0, s] + 1, label)
-        return source, label
+        found[0, p] = source
+        found[1, p] = label
+        return carry
 
     def pack_label(p, carry):
-        _, label = source_of(p)
-        lab_send[p] = jnp.full((1, 128), label, jnp.int32)
+        lab_send[p] = jnp.full((1, 128), found[1, p], jnp.int32)
         return carry
 
     def pack_image(p, carry):
-        source, _ = source_of(p)
-        img_send[p] = img_in[source]
+        img_send[p] = img_in[found[0, p]]
         return carry
 
     def pack_weight(p, carry):
-        source, _ = source_of(p)
-        wgt_send[p] = wgt_in[source]
+        wgt_send[p] = wgt_in[found[0, p]]
         return carry
 
     def other_patch(i):
-        step = lax.select(lax.rem(i, 2) == 0, patches // 2 + lax.div(i, 2), lax.div(i + 1, 2))
+        step = lax.select(lax.rem(i, 2) == 0, patches - 1 - lax.div(i, 2), lax.div(i + 1, 2))
         other, bit = jnp.int32(0), 1
         while bit < patches:
             other = other + bit * lax.rem(lax.div(me, bit) + lax.div(step, bit), 2)
@@ -128,7 +127,7 @@
 
     loads[4].wait()
     loads[5].wait()
-    lax.fori_loop(0, patches, pack_label, 0)
+    lax.fori_loop(0, patches, find, 0)
     loads[0].wait()
     lax.fori_loop(0, patches, pack_image, 0)
     pl.semaphore_wait(barrier, devices - 1)
@@ -151,6 +150,7 @@
 
     first = patches // 2
     lax.fori_loop(0, first, functools.partial(send_image, sem=img_fsem), 0)
+    lax.fori_loop(0, patches, pack_label, 0)
     lax.fori_loop(0, patches - 1, send_label, 0)
     pltpu.make_async_copy(lab_send.at[me], lab_recv.at[my_group, me], lab_rsem).start()
     lax.fori_loop(first, patches - 1, send_image, 0)
@@ -321,11 +321,11 @@
             out_shape=pltpu.VMEM((1, slab, cols), F32),
             in_specs=[far] * 7,
             out_specs=pl.BlockSpec(memory_space=pltpu.VMEM),
-
             scratch_shapes=[
                 pltpu.SMEM(strip_patch.shape, jnp.int32),
                 pltpu.SMEM(strip_slot.shape, jnp.int32),
                 pltpu.SMEM(coef.shape, F32),
+                pltpu.SMEM((2, patches), jnp.int32),
                 pltpu.VMEM((strips, rows, width), BF16),
                 pltpu.VMEM((strips, rows, width), BF16),
                 pltpu.VMEM(vertical.shape, F32),

time: 31.9 us -> 33.7 us (1.056)
  the two profiles are of different devices: /device:TPU:9 before, /device:TPU:0 now
where the time goes in v5:
time: 33.7 us; the launch traced here: 33.6 us
  Pallas kernels  32.9 us (98%)
  local copies, waits for them, and re-layouts  0.66 us (2%)
    pallas_call x1, Pallas kernels, per_device(): pl.pallas_call(functools.partial(kernel, groups, patches), out_shape=pltp...  32.9 us

profile of v5, /device:TPU:0, one launch (start us, length us, event | category | flops | bytes accessed | tf_op | source)
XLA Modules:
  0.0 33.6 jit_solution(10243994379874957403)
XLA Ops:
  0.0 32.9 %shard_map.73 = f32[1,64,512]{2,1,0:T(8,128)S(1)} custom-call(s32[1,8]{1,0:T(1,128)} %patch_hbm.1, s32[1,8]{1,0:T(1,128)} %slot_hbm.1, f32[3,2,31]{2,1,0:T(2,128)} %bitcast.3, bf16[1,8,128,128]{3,2,1,0:T(8,128)(2,1)} %img_hbm.1, bf16[1,8,128,128]{3,2,1,0:T(8,128)(2,1)} %wgt_hbm.1, f32[12,128,128]{2,1,0:T(8,128)} %constant.4.clone.ver_hbm, ...), custom_call_target="tpu_custom_call" | custom-call | flops 1610612736 | bytes 2097152 | tf_op jit(solution)/shard_map/pallas_call | solution.py:319
  32.9 0.7 %copy.9 = f32[1,64,512]{2,1,0:T(8,128)} copy(f32[1,64,512]{2,1,0:T(8,128)S(1)} %shard_map.73) | data formatting | bytes 262144

commit v6 on v5

--- a/solution.py
+++ b/solution.py
@@ -118,7 +118,14 @@
         return carry
 
     def other_patch(i):
-        step = lax.select(lax.rem(i, 2) == 0, patches - 1 - lax.div(i, 2), lax.div(i + 1, 2))
+        quarter = patches // 4
+        lead = quarter // 2
+        j = lax.div(i, 2)
+        by_turns = lax.select(
+            lax.rem(j - lead + quarter, 2) == 0, quarter + lax.div(j - lead, 2), lead + lax.div(j - lead, 2)
+        )
+        far = lax.select(j < lead, j, lax.select(j >= quarter + lead, j, by_turns))
+        step = lax.select(lax.rem(i, 2) == 0, 2 * quarter + far, j + 1)
         other, bit = jnp.int32(0), 1
         while bit < patches:
             other = other + bit * lax.rem(lax.div(me, bit) + lax.div(step, bit), 2)

time: 33.7 us -> 31.4 us (0.932); the launches traced: 33.6 us -> 30.9 us
  Pallas kernels: 32.9 us -> 30.2 us
    pallas_call x1, Pallas kernels: 32.9 us -> 30.2 us  [per_device(): pl.pallas_call(functools.partial(kernel, groups, patches), out_shape=pltp...]
where the time goes in v6:
time: 31.4 us; the launch traced here: 30.9 us
  Pallas kernels  30.2 us (96%)
  local copies, waits for them, and re-layouts  0.66 us (2%)
    pallas_call x1, Pallas kernels, per_device(): pl.pallas_call(functools.partial(kernel, groups, patches), out_shape=pltp...  30.2 us
    unnamed x1, local copies, waits for them, and re-layouts  0.66 us

profile of v6, /device:TPU:0, one launch (start us, length us, event | category | flops | bytes accessed | tf_op | source)
XLA Modules:
  0.0 30.9 jit_solution(8210453933400137290)
XLA Ops:
  0.0 30.2 %shard_map.73 = f32[1,64,512]{2,1,0:T(8,128)S(1)} custom-call(s32[1,8]{1,0:T(1,128)} %patch_hbm.1, s32[1,8]{1,0:T(1,128)} %slot_hbm.1, f32[3,2,31]{2,1,0:T(2,128)} %bitcast.3, bf16[1,8,128,128]{3,2,1,0:T(8,128)(2,1)} %img_hbm.1, bf16[1,8,128,128]{3,2,1,0:T(8,128)(2,1)} %wgt_hbm.1, f32[12,128,128]{2,1,0:T(8,128)} %constant.4.clone.ver_hbm, ...), custom_call_target="tpu_custom_call" | custom-call | flops 1610612736 | bytes 2097152 | tf_op jit(solution)/shard_map/pallas_call | solution.py:326
  30.2 0.7 %copy.9 = f32[1,64,512]{2,1,0:T(8,128)} copy(f32[1,64,512]{2,1,0:T(8,128)S(1)} %shard_map.73) | data formatting | bytes 262144

commit v7 on v6

--- a/solution.py
+++ b/solution.py
@@ -194,7 +194,7 @@
         return pl.ds(pl.multiple_of(g * slab, slab), slab)
 
     def send_weight(i, carry):
-        p = other_patch(i)
+        p = other_patch(lax.select(i < first, 2 * i, 2 * (i - first) + 1))
         for d in range(groups):
             g = lax.rem(my_group + d, groups)
             pltpu.make_async_remote_copy(

time: 31.4 us -> 32.1 us (1.022); the launches traced: 30.9 us -> 31.9 us
  Pallas kernels: 30.2 us -> 31.3 us
    pallas_call x1, Pallas kernels: 30.2 us -> 31.3 us  [per_device(): pl.pallas_call(functools.partial(kernel, groups, patches), out_shape=pltp...]
where the time goes in v7:
time: 32.1 us; the launch traced here: 31.9 us
  Pallas kernels  31.3 us (98%)
  local copies, waits for them, and re-layouts  0.66 us (2%)
    pallas_call x1, Pallas kernels, per_device(): pl.pallas_call(functools.partial(kernel, groups, patches), out_shape=pltp...  31.3 us
    unnamed x1, local copies, waits for them, and re-layouts  0.66 us

profile of v7, /device:TPU:0, one launch (start us, length us, event | category | flops | bytes accessed | tf_op | source)
XLA Modules:
  0.0 31.9 jit_solution(13426130327614737401)
XLA Ops:
  0.0 31.3 %shard_map.73 = f32[1,64,512]{2,1,0:T(8,128)S(1)} custom-call(s32[1,8]{1,0:T(1,128)} %patch_hbm.1, s32[1,8]{1,0:T(1,128)} %slot_hbm.1, f32[3,2,31]{2,1,0:T(2,128)} %bitcast.3, bf16[1,8,128,128]{3,2,1,0:T(8,128)(2,1)} %img_hbm.1, bf16[1,8,128,128]{3,2,1,0:T(8,128)(2,1)} %wgt_hbm.1, f32[12,128,128]{2,1,0:T(8,128)} %constant.4.clone.ver_hbm, ...), custom_call_target="tpu_custom_call" | custom-call | flops 1610612736 | bytes 2097152 | tf_op jit(solution)/shard_map/pallas_call | solution.py:326
  31.3 0.7 %copy.9 = f32[1,64,512]{2,1,0:T(8,128)} copy(f32[1,64,512]{2,1,0:T(8,128)S(1)} %shard_map.73) | data formatting | bytes 262144

commit v8 on v7

--- a/solution.py
+++ b/solution.py
@@ -194,7 +194,8 @@
         return pl.ds(pl.multiple_of(g * slab, slab), slab)
 
     def send_weight(i, carry):
-        p = other_patch(lax.select(i < first, 2 * i, 2 * (i - first) + 1))
+        near = first - 1
+        p = other_patch(lax.select(i < near, 2 * i + 1, 2 * (i - near)))
         for d in range(groups):
             g = lax.rem(my_group + d, groups)
             pltpu.make_async_remote_copy(

time: 32.1 us -> 31 us (0.966)
  Pallas kernels: 31.3 us -> 30.2 us
    pallas_call x1, Pallas kernels: 31.3 us -> 30.2 us  [per_device(): pl.pallas_call(functools.partial(kernel, groups, patches), out_shape=pltp...]
where the time goes in v8:
time: 31 us; the launch traced here: 30.9 us
  Pallas kernels  30.2 us (97%)
  local copies, waits for them, and re-layouts  0.66 us (2%)
    pallas_call x1, Pallas kernels, per_device(): pl.pallas_call(functools.partial(kernel, groups, patches), out_shape=pltp...  30.2 us
    unnamed x1, local copies, waits for them, and re-layouts  0.66 us

profile of v8, /device:TPU:0, one launch (start us, length us, event | category | flops | bytes accessed | tf_op | source)
XLA Modules:
  0.0 30.9 jit_solution(11369716800980504424)
XLA Ops:
  0.0 30.2 %shard_map.73 = f32[1,64,512]{2,1,0:T(8,128)S(1)} custom-call(s32[1,8]{1,0:T(1,128)} %patch_hbm.1, s32[1,8]{1,0:T(1,128)} %slot_hbm.1, f32[3,2,31]{2,1,0:T(2,128)} %bitcast.3, bf16[1,8,128,128]{3,2,1,0:T(8,128)(2,1)} %img_hbm.1, bf16[1,8,128,128]{3,2,1,0:T(8,128)(2,1)} %wgt_hbm.1, f32[12,128,128]{2,1,0:T(8,128)} %constant.4.clone.ver_hbm, ...), custom_call_target="tpu_custom_call" | custom-call | flops 1610612736 | bytes 2097152 | tf_op jit(solution)/shard_map/pallas_call | solution.py:327
  30.2 0.7 %copy.9 = f32[1,64,512]{2,1,0:T(8,128)} copy(f32[1,64,512]{2,1,0:T(8,128)S(1)} %shard_map.73) | data formatting | bytes 262144

commit v9 on v8

--- a/solution.py
+++ b/solution.py
@@ -119,12 +119,12 @@
 
     def other_patch(i):
         quarter = patches // 4
-        lead = quarter // 2
+        lead = quarter - quarter // 4
         j = lax.div(i, 2)
         by_turns = lax.select(
             lax.rem(j - lead + quarter, 2) == 0, quarter + lax.div(j - lead, 2), lead + lax.div(j - lead, 2)
         )
-        far = lax.select(j < lead, j, lax.select(j >= quarter + lead, j, by_turns))
+        far = lax.select(j < lead, j, lax.select(j >= 2 * quarter - lead, j, by_turns))
         step = lax.select(lax.rem(i, 2) == 0, 2 * quarter + far, j + 1)
         other, bit = jnp.int32(0), 1
         while bit < patches:
@@ -148,19 +148,20 @@
         return carry
 
     def send_image(i, carry, sem=img_ssem):
-        p = other_patch(i)
+        p = other_patch(lax.select(i < patches // 2, 2 * i, 2 * (i - patches // 2) + 1))
         pltpu.make_async_remote_copy(
             src_ref=img_send.at[p], dst_ref=img_recv.at[me],
             send_sem=sem, recv_sem=img_rsem, device_id=(my_group, p), device_id_type=MESH,
         ).start()
         return carry
 
-    first = patches // 2
+    first = patches // 4
     lax.fori_loop(0, first, functools.partial(send_image, sem=img_fsem), 0)
+    lax.fori_loop(first, 2 * first, send_image, 0)
     lax.fori_loop(0, patches, pack_label, 0)
     lax.fori_loop(0, patches - 1, send_label, 0)
     pltpu.make_async_copy(lab_send.at[me], lab_recv.at[my_group, me], lab_rsem).start()
-    lax.fori_loop(first, patches - 1, send_image, 0)
+    lax.fori_loop(2 * first, patches - 1, send_image, 0)
     pltpu.make_async_copy(img_send.at[me], img_recv.at[me], img_rsem).start()
 
     loads[1].wait()
@@ -194,7 +195,7 @@
         return pl.ds(pl.multiple_of(g * slab, slab), slab)
 
     def send_weight(i, carry):
-        near = first - 1
+        near = patches // 2 - 1
         p = other_patch(lax.select(i < near, 2 * i + 1, 2 * (i - near)))
         for d in range(groups):
             g = lax.rem(my_group + d, groups)

time: 31 us -> 30.3 us (0.977)
  Pallas kernels: 30.2 us -> 29.5 us
    pallas_call x1, Pallas kernels: 30.2 us -> 29.5 us  [per_device(): pl.pallas_call(functools.partial(kernel, groups, patches), out_shape=pltp...]
where the time goes in v9:
time: 30.3 us; the launch traced here: 30.2 us
  Pallas kernels  29.5 us (97%)
  local copies, waits for them, and re-layouts  0.66 us (2%)
    pallas_call x1, Pallas kernels, per_device(): pl.pallas_call(functools.partial(kernel, groups, patches), out_shape=pltp...  29.5 us
    unnamed x1, local copies, waits for them, and re-layouts  0.66 us

profile of v9, /device:TPU:0, one launch (start us, length us, event | category | flops | bytes accessed | tf_op | source)
XLA Modules:
  0.0 30.2 jit_solution(3151673572448886640)
XLA Ops:
  0.0 29.5 %shard_map.73 = f32[1,64,512]{2,1,0:T(8,128)S(1)} custom-call(s32[1,8]{1,0:T(1,128)} %patch_hbm.1, s32[1,8]{1,0:T(1,128)} %slot_hbm.1, f32[3,2,31]{2,1,0:T(2,128)} %bitcast.3, bf16[1,8,128,128]{3,2,1,0:T(8,128)(2,1)} %img_hbm.1, bf16[1,8,128,128]{3,2,1,0:T(8,128)(2,1)} %wgt_hbm.1, f32[12,128,128]{2,1,0:T(8,128)} %constant.4.clone.ver_hbm, ...), custom_call_target="tpu_custom_call" | custom-call | flops 1610612736 | bytes 2097152 | tf_op jit(solution)/shard_map/pallas_call | solution.py:328
  29.5 0.7 %copy.9 = f32[1,64,512]{2,1,0:T(8,128)} copy(f32[1,64,512]{2,1,0:T(8,128)S(1)} %shard_map.73) | data formatting | bytes 262144

commit v10 on v9

--- a/solution.py
+++ b/solution.py
@@ -189,7 +189,6 @@
 
     lax.fori_loop(0, visits, mix_visit, 0)
 
-    pltpu.make_async_copy(img_send.at[pl.ds(0, first)], img_send.at[pl.ds(0, first)], img_fsem).wait()
 
     def slab_of(g):
         return pl.ds(pl.multiple_of(g * slab, slab), slab)
@@ -302,6 +301,7 @@
         out_ref[0, :, here] = numer / denom
 
     some = pl.ds(0, patches - 1)
+    pltpu.make_async_copy(img_send.at[pl.ds(0, first)], img_send.at[pl.ds(0, first)], img_fsem).wait()
     last = pl.ds(0, patches - 1 - first)
     pltpu.make_async_copy(img_send.at[last], img_send.at[last], img_ssem).wait()
     pltpu.make_async_copy(lab_send.at[some], lab_send.at[some], lab_ssem).wait()

time: 30.3 us -> 30.3 us (level)
  no operation moved by 1% of the time
where the time goes in v10:
time: 30.3 us; the launch traced here: 30.2 us
  Pallas kernels  29.5 us (97%)
  local copies, waits for them, and re-layouts  0.66 us (2%)
    pallas_call x1, Pallas kernels, per_device(): pl.pallas_call(functools.partial(kernel, groups, patches), out_shape=pltp...  29.5 us
    unnamed x1, local copies, waits for them, and re-layouts  0.66 us

profile of v10, /device:TPU:0, one launch (start us, length us, event | category | flops | bytes accessed | tf_op | source)
XLA Modules:
  0.0 30.2 jit_solution(15199270798162351784)
XLA Ops:
  0.0 29.5 %shard_map.73 = f32[1,64,512]{2,1,0:T(8,128)S(1)} custom-call(s32[1,8]{1,0:T(1,128)} %patch_hbm.1, s32[1,8]{1,0:T(1,128)} %slot_hbm.1, f32[3,2,31]{2,1,0:T(2,128)} %bitcast.3, bf16[1,8,128,128]{3,2,1,0:T(8,128)(2,1)} %img_hbm.1, bf16[1,8,128,128]{3,2,1,0:T(8,128)(2,1)} %wgt_hbm.1, f32[12,128,128]{2,1,0:T(8,128)} %constant.4.clone.ver_hbm, ...), custom_call_target="tpu_custom_call" | custom-call | flops 1610612736 | bytes 2097152 | tf_op jit(solution)/shard_map/pallas_call | solution.py:328
  29.5 0.7 %copy.9 = f32[1,64,512]{2,1,0:T(8,128)} copy(f32[1,64,512]{2,1,0:T(8,128)S(1)} %shard_map.73) | data formatting | bytes 262144
